TPU v7x, 32 devices: a whole 2x2x4 slice. The times are simulated.
32 devices in a mesh: wide: 16 (over z, x, core), narrow: 2 (over y).
Axes of the slice: x: 2, y: 2, z: 4, core: 2. Of those that a mesh axis runs over, the one named last changes fastest.
Arguments:
- tokens: bfloat16 [32, 1024, 768], P(('wide', 'narrow')), may hold values from -6 to 6
- lengths: int32 [32, 4], P(('wide', 'narrow')), may hold values from 1 to 512, 1024 in all within a row
- cotangent: bfloat16 [32, 1024, 768], P(('wide', 'narrow')), may hold values from -6 to 6
- vectors: bfloat16 [11, 768], P(None, ('wide', 'narrow')), may hold values from -6 to 3, as said below
- time_recept: bfloat16 [589824], P(('wide', 'narrow')), may hold values from -0.21875 to 0.21875
- time_key: bfloat16 [589824], P(('wide', 'narrow')), may hold values from -0.21875 to 0.21875
- time_value: bfloat16 [589824], P(('wide', 'narrow')), may hold values from -0.21875 to 0.21875
- time_output: bfloat16 [589824], P(('wide', 'narrow')), may hold values from -1.25 to 1.25
- channel_key: bfloat16 [2359296], P(('wide', 'narrow')), may hold values from -0.21875 to 0.21875
- channel_value: bfloat16 [2359296], P(('wide', 'narrow')), may hold values from -0.109375 to 0.109375
- channel_recept: bfloat16 [589824], P(('wide', 'narrow')), may hold values from -0.21875 to 0.21875
Outputs:
- result: bfloat16 [32, 1024, 768], P(('wide', 'narrow'))
- input_grad: bfloat16 [32, 1024, 768], P(('wide', 'narrow'))
- vectors_grad: float32 [11, 768], P(None, ('wide', 'narrow'))
- time_recept_grad: float32 [589824], P(('wide', 'narrow'))
- time_key_grad: float32 [589824], P(('wide', 'narrow'))
- time_value_grad: float32 [589824], P(('wide', 'narrow'))
- time_output_grad: float32 [589824], P(('wide', 'narrow'))
- channel_key_grad: float32 [2359296], P(('wide', 'narrow'))
- channel_value_grad: float32 [2359296], P(('wide', 'narrow'))
- channel_recept_grad: float32 [589824], P(('wide', 'narrow'))
Inputs may be any that keep to these rules, and one draw needn't show every extreme that they name: Each row's 4 document lengths sum to 1024; each row's longest document has 512 tokens. `vectors`: the gains lie in [0.5, 1.5], the biases in [-0.5, 0.5], the five mix rows in [0, 1], decay in [-6, 3] and bonus in [-1.5, 1.5].
All inputs are finite; a program needn't handle non-finite values.
Results may differ from a plain program's by a relative error of at most 0.0085.
Values may be sent and summed in bfloat16 or wider, within the bound.
A program may use at most 256 MiB of HBM per device.

v0:
```python
from functools import partial

import jax
import jax.numpy as jnp
from jax import lax
from jax.experimental import pallas as pl
from jax.experimental.pallas import tpu as pltpu
from jax.sharding import PartitionSpec as P


SEG = 16
LANES = 128
EPS = 1e-05
F32 = jnp.float32
BF16 = jnp.bfloat16
VMEM_LIMIT = 63 * 1024 * 1024


def wide_of(column, width):
    return jnp.concatenate([column] * (width // LANES), axis=1)


def dot_nn(left, right):
    return jnp.dot(left, right, preferred_element_type=F32)


def dot_nt(left, right):
    return lax.dot_general(left, right, (((1,), (1,)), ((), ())), preferred_element_type=F32)


def dot_tn(left, right):
    return lax.dot_general(left, right, (((0,), (0,)), ((), ())), preferred_element_type=F32)


def local(source, target, sem):
    return pltpu.make_async_copy(source, target, sem)


def rows_at(index, size):
    return pl.ds(pl.multiple_of(index * size, size), size)


def fill_mask(lengths, mask, length):
    steps = length // SEG

    @pl.loop(0, length // 128)
    def _(block):
        row = block * 128 + lax.broadcasted_iota(jnp.int32, (128, LANES), 0)
        place = (row % SEG) * steps + row // SEG
        start = jnp.int32(0)
        fresh = place == 0
        for doc in range(lengths.shape[1] - 1):
            start = start + lengths[0, doc]
            fresh = jnp.logical_or(fresh, place == start)
        mask[rows_at(block, 128), :] = jnp.where(fresh, 0.0, 1.0)


def widen(source, target):
    @pl.loop(0, source.shape[0] // 32)
    def _(block):
        rows = rows_at(block, 32)
        for c in range(target.shape[0]):
            target[c, rows, :] = source[rows, c * LANES : (c + 1) * LANES].astype(F32)


def narrow(source, target):
    @pl.loop(0, target.shape[0] // 32)
    def _(block):
        rows = rows_at(block, 32)
        for c in range(source.shape[0]):
            target[rows, c * LANES : (c + 1) * LANES] = source[c, rows, :].astype(BF16)


def take_step(source, step, steps):
    strip = pl.ds(step, SEG, stride=steps)
    return jnp.concatenate([source[c, strip, :] for c in range(source.shape[0])], axis=1)


def put_step(target, step, steps, rows):
    strip = pl.ds(step, SEG, stride=steps)
    for c in range(target.shape[0]):
        target[c, strip, :] = rows[:, c * LANES : (c + 1) * LANES]


def take_rows(source, rows):
    return jnp.concatenate([source[c, rows, :] for c in range(source.shape[0])], axis=1)


def put_rows(target, rows, value):
    for c in range(target.shape[0]):
        target[c, rows, :] = value[:, c * LANES : (c + 1) * LANES]


def norm_rows(rows):
    centred = rows - jnp.mean(rows, axis=-1, keepdims=True)
    scale = lax.rsqrt(jnp.mean(centred * centred, axis=-1, keepdims=True) + EPS)
    return centred * scale, scale


def join_runs(local_end, through, backward):
    index = lax.broadcasted_iota(jnp.int32, local_end[0].shape, 0)
    if backward:
        index = SEG - 1 - index
    states = list(local_end)
    hop = 1
    while hop < SEG:
        turn = SEG - hop if backward else hop
        inside = index >= hop
        moved = pltpu.roll(through, turn, 0)
        states = [jnp.where(inside, s + through * pltpu.roll(s, turn, 0), s) for s in states]
        through = jnp.where(inside, through * moved, through)
        hop *= 2
    turn = SEG - 1 if backward else 1
    return [jnp.where(index >= 1, pltpu.roll(s, turn, 0), 0.0) for s in states]


class Place:
    def __init__(self):
        index = lax.axis_index("wide")
        self.z, self.x, self.c = index // 4, index // 2 % 2, index % 2
        self.y = lax.axis_index("narrow")

    def at(self, z=None, x=None, c=None, y=None):
        z, x = self.z if z is None else z, self.x if x is None else x
        c, y = self.c if c is None else c, self.y if y is None else y
        return (z * 4 + x * 2 + c, y)

    def along_z(self, hop):
        return (self.z + hop) % 4

    def partners(self):
        return [self.at(z=self.along_z(hop)) for hop in (1, 2, 3)] + [
            self.at(x=1 - self.x), self.at(y=1 - self.y), self.at(c=1 - self.c)
        ]


def greet(place):
    barrier = pltpu.get_barrier_semaphore()
    partners = place.partners()
    for partner in partners:
        pl.semaphore_signal(barrier, inc=1, device_id=partner, device_id_type=pl.DeviceIdType.MESH)
    pl.semaphore_wait(barrier, len(partners))


def remote(source, target, send, recv, device):
    return pltpu.make_async_remote_copy(
        src_ref=source, dst_ref=target, send_sem=send, recv_sem=recv,
        device_id=device, device_id_type=pl.DeviceIdType.MESH,
    )


class Gather:
    def __init__(self, place, piece, half_cols, order, send, recv):
        every = slice(None)
        p, (z, x, c) = place, (place.z, place.x, place.c)
        spans = []
        mine = piece(z, x, c, half_cols)
        spans.append([(mine, p.at(z=p.along_z(hop))) for hop in (1, 2, 3)])
        if order == "xy":
            spans.append([(piece(every, x, c, half_cols), p.at(x=1 - x))])
            spans.append([(piece(every, every, c, half_cols), p.at(y=1 - p.y))])
        else:
            spans.append([(piece(every, x, c, half_cols), p.at(y=1 - p.y))])
            spans.append([(piece(every, x, c, every), p.at(x=1 - x))])
        spans.append([(piece(every, every, c, every), p.at(c=1 - c))])
        self.phases, number = [], 0
        for span in spans:
            copies = []
            for ref, device in span:
                copies.append(remote(ref, ref, send.at[number], recv.at[number], device))
                number += 1
            self.phases.append(copies)

    def start(self, phase):
        for copy in self.phases[phase]:
            copy.start()

    def arrive(self, phase):
        for copy in self.phases[phase]:
            copy.wait_recv()

    def step(self, phase):
        if phase:
            self.arrive(phase - 1)
        if phase < len(self.phases):
            self.start(phase)

    def finish(self):
        for copies in self.phases:
            for copy in copies:
                copy.wait_send()


def join_vectors(tiles, vec, share):
    width = vec.shape[1]
    lane = lax.broadcasted_iota(jnp.int32, (16, LANES), 1)
    blocks = [jnp.zeros((16, LANES), F32) for _ in range(width // LANES)]
    for index in range(width // share):
        z, x, c, y = index // 8, index // 4 % 2, index // 2 % 2, index % 2
        block, shift = index * share // LANES, index * share % LANES
        tile = tiles[z, x, c, y]
        tile = pltpu.roll(tile, shift, 1) if shift else tile
        if shift + share > LANES:
            blocks[block] += jnp.where(lane >= shift, tile, 0.0)
            blocks[block + 1] += jnp.where(lane < shift, tile, 0.0)
        else:
            blocks[block] += tile
    for block, tile in enumerate(blocks):
        vec[:, block * LANES : (block + 1) * LANES] = tile


class Gathers:
    GROUPS = (
        (("4", 1, 1, "xy"), ("4", 2, 1, "yx")),
        (("4", 0, 1, "xy"), ("4", 3, 1, "yx")),
        (("k", 0, 1, "xy"), ("k", 1, 1, "yx")),
        (("k", 2, 1, "xy"), ("k", 3, 1, "yx")),
        (("g", 0, 1, "xy"),),
        (("v", 0, 1, "yx"), ("v", 1, 1, "xy")),
        (("v", 2, 1, "yx"), ("v", 3, 1, "xy")),
    )
    AHEAD = 0

    def __init__(self, shards, stages, weights, tile_in, tiles, vec, share, send, recv):
        self.place = place = Place()
        self.shards, self.stages, self.weights = shards, stages, weights
        self.tile_in, self.tiles, self.vec, self.share = tile_in, tiles, vec, share
        half = weights["4"].shape[-1] // 2
        self.cols = pl.ds(pl.multiple_of(place.y * half, half), half)
        self.halves = {
            name: remote(shards[name].at[1 - place.y], stages[name], send.at[0, i], recv.at[0, i], place.at(y=1 - place.y))
            for i, name in enumerate("4kvg")
        }
        self.vectors = Gather(
            place, lambda z, x, c, y: tiles.at[z, x, c, y], place.y, "xy", send.at[1], recv.at[1]
        )
        self.groups, number = [], 2
        for members in self.GROUPS:
            group = []
            for name, first, count, order in members:

                def piece(z, x, c, cols, ref=weights[name], first=first, count=count):
                    return ref.at[z, x, c, pl.ds(first, count), :, cols]

                group.append(Gather(place, piece, self.cols, order, send.at[number], recv.at[number]))
                number += 1
            self.groups.append(group)

    def begin(self):
        place = self.place
        self.tiles[place.z, place.x, place.c, place.y] = self.tile_in[...]
        greet(place)
        self.vectors.start(0)
        for name in "4kvg":
            self.halves[name].start()

    def merge(self):
        place, y = self.place, self.place.y
        for name in "4kgv":
            self.halves[name].wait_recv()
            slab = self.weights[name].at[place.z, place.x, place.c]
            mine, theirs = self.shards[name].at[y], self.stages[name]
            for q in range(mine.shape[0]):
                if name == "v":
                    slab[2 * y + q, :, self.cols] = mine[q]
                    slab[2 * (1 - y) + q, :, self.cols] = theirs[q]
                else:
                    one, two = mine[q].astype(F32), theirs[q].astype(F32)
                    upper, lower = jnp.where(y == 0, one, two), jnp.where(y == 0, two, one)
                    slab[q, :, self.cols] = jnp.concatenate([upper, lower], axis=0).astype(BF16)
            if name == "4":
                self.stage(0)

    def stage(self, number):
        for index, group in enumerate(self.groups):
            if 1 <= number - index <= 4:
                for piece in group:
                    piece.arrive(number - index - 1)
                for piece in group:
                    if number - index < 4:
                        piece.start(number - index)
            early = max(index - self.AHEAD, 0)
            if number == early:
                for piece in group:
                    piece.start(0)

    def finish(self):
        self.vectors.finish()
        for name in "4kvg":
            self.halves[name].wait_send()
        for group in self.groups:
            for piece in group:
                piece.finish()


class Scatter:
    def __init__(self, place, cols, grad, ways, send, recv):
        p, (mine, other), every = place, cols, slice(None)
        self.place, self.mine, self.grad = place, mine, grad
        self.sum, self.first, self.second, self.third, self.y_first = ways
        total, x = self.sum, p.x
        copies = [[remote(grad.at[:, :, 1 - p.c], total, send.at[0], recv.at[0], p.at(c=1 - p.c))]]
        if self.y_first:
            one, to_one = total.at[:, :, :, other], p.at(y=1 - p.y)
            two, to_two = total.at[:, 1 - x, :, mine], p.at(x=1 - x)
        else:
            one, to_one = total.at[:, 1 - x], p.at(x=1 - x)
            two, to_two = total.at[:, x, :, other], p.at(y=1 - p.y)
        copies.append([remote(one, self.first, send.at[1], recv.at[1], to_one)])
        copies.append([remote(two, self.second, send.at[2], recv.at[2], to_two)])
        copies.append([
            remote(total.at[p.along_z(hop), x, :, mine], self.third.at[hop - 1], send.at[2 + hop], recv.at[2 + hop],
                   p.at(z=p.along_z(hop)))
            for hop in (1, 2, 3)
        ])
        self.copies = copies

    def start(self, phase):
        for copy in self.copies[phase]:
            copy.start()

    def sent(self, *phases):
        for phase in phases:
            for copy in self.copies[phase]:
                copy.wait_send()

    def step(self, number):
        if number:
            for copy in self.copies[number - 1]:
                copy.wait_recv()
        p, total, mine = self.place, self.sum, self.mine
        if number == 1:

            @pl.loop(0, 4)
            def _(z):
                for x in range(2):
                    total[z, x] += self.grad[z, x, p.c]

        if number == 2:

            @pl.loop(0, 4)
            def _(z):
                if self.y_first:
                    for x in range(2):
                        total[z, x, :, mine] += self.first[z, x]
                else:
                    total[z, p.x] += self.first[z]

        if number == 3:

            @pl.loop(0, 4)
            def _(z):
                total[z, p.x, :, mine] += self.second[z]

        if number < 4:
            self.start(number)

    def result(self):
        p = self.place
        total = self.sum[p.z, p.x, :, self.mine].astype(F32)
        for hop in range(3):
            total += self.third[hop].astype(F32)
        return total


class Scatters:
    SLOTS = {"v": (0, 1, 2, 3), "4": (0, 1, 2, 3), "k": (4, 5, 6, 7), "g": (8,)}

    def __init__(self, grad, grad_gate, outs, ways, finals, arrived, sums, send, recv, free):
        self.place = place = Place()
        self.outs, self.finals, self.arrived, self.sums, self.free = outs, finals, arrived, sums, free
        half = grad.shape[-1] // 2
        mine = pl.ds(pl.multiple_of(place.y * half, half), half)
        other = pl.ds(pl.multiple_of((1 - place.y) * half, half), half)
        self.mine, self.other = mine, other
        total, first_y, first_x, second, third = ways
        self.pieces, number = {}, 0
        for name, slots in self.SLOTS.items():
            source = grad_gate if name == "g" else grad
            for q, slot in enumerate(slots):
                y_first = slot % 2 == 0
                first = (first_y if y_first else first_x).at[slot // 2]
                way = (total.at[slot], first, second.at[slot], third.at[slot], y_first)
                self.pieces[name, q] = Scatter(
                    place, (mine, other), source.at[:, :, :, q], way, send.at[number], recv.at[number]
                )
                number += 1
        self.last = {
            name: remote(finals[name], arrived[name], send.at[number, i], recv.at[number, i], place.at(y=1 - place.y))
            for i, name in enumerate("4kvg")
        }
        number += 1
        to = [place.at(c=1 - place.c), place.at(y=1 - place.y), place.at(x=1 - place.x)]
        self.hops = [
            [remote(sums.at[i], sums.at[4 + i], send.at[number, i], recv.at[number, i], device)]
            for i, device in enumerate(to)
        ]
        self.hops.append([
            remote(sums.at[3], sums.at[6 + hop], send.at[number, 2 + hop], recv.at[number, 2 + hop],
                   place.at(z=place.along_z(hop)))
            for hop in (1, 2, 3)
        ])

    def step(self, name, qs, number):
        for q in qs:
            self.pieces[name, q].step(number)

    def close(self, name, qs):
        y = self.place.y
        for q in qs:
            piece = self.pieces[name, q]
            piece.step(4)
            total = piece.result()
            if name == "v":

                @pl.when(y == q // 2)
                def _():
                    self.outs[name][q % 2, :, self.mine] = total

                @pl.when(y != q // 2)
                def _():
                    self.finals[name][q % 2] = total.astype(BF16)
            else:
                half = total.shape[0] // 2
                upper, lower = total[:half], total[half:]
                self.outs[name][q, :, self.mine] = jnp.where(y == 0, upper, lower)
                self.finals[name][q] = jnp.where(y == 0, lower, upper).astype(BF16)

    def send_rows(self, name):
        self.last[name].start()

    def take_rows(self, name):
        self.last[name].wait_recv()
        self.outs[name][:, :, self.other] = self.arrived[name][...].astype(F32)

    def release(self):
        for q in range(4):
            self.pieces["v", q].sent(1, 2, 3)
        for partner in self.place.partners():
            pl.semaphore_signal(self.free, inc=1, device_id=partner, device_id_type=pl.DeviceIdType.MESH)

    def claim(self):
        pl.semaphore_wait(self.free, 6)

    def hop(self, number):
        if number:
            for copy in self.hops[number - 1]:
                copy.wait_recv()
        if 1 <= number <= 3:
            self.sums[number] = self.sums[number - 1] + self.sums[3 + number]
        if number < 4:
            for copy in self.hops[number]:
                copy.start()

    def finish(self):
        for (name, _), piece in self.pieces.items():
            if name == "v":
                continue
            piece.sent(1, 2, 3)
            if name != "k":
                piece.sent(0)
        for copy in self.last.values():
            copy.wait_send()
        for copies in self.hops:
            for copy in copies:
                copy.wait_send()


def forward_kernel(share, *refs):
    lengths, tokens, cotangent, vec_in, w4_in, wk_in, wv_in, wg_in = refs[:8]
    result, n1_out, n2_out, r_out, mix_out, state_out, key_out, att_out, cig_out, sq_out, gsg_out, up_out = refs[8:20]
    length, width = tokens.shape
    steps = length // SEG
    if share:
        w4_out, wk_out, wv_out, wg_out, vec_out = refs[20:25]
        w4, wk, wv, wg, nat, norm, mid, state, keys, half, sq, mask, rsd, sems = refs[25:39]
        stage4, stagek, stagev, stageg, tiles, vec, send, recv = refs[39:]
        gathers = Gathers(
            {"4": w4_in, "k": wk_in, "v": wv_in, "g": wg_in},
            {"4": stage4, "k": stagek, "v": stagev, "g": stageg},
            {"4": w4, "k": wk, "v": wv, "g": wg},
            vec_in, tiles, vec, share, send, recv,
        )
    else:
        w4, wk, wv, wg, nat, norm, mid, state, keys, half, sq, mask, rsd, sems = refs[20:]
        vec, gathers = vec_in, None

    def stage(number):
        if gathers:
            gathers.stage(number)

    load_tok = local(tokens, half.at[0], sems.at[0])
    load_cot = local(cotangent, half.at[1], sems.at[1])
    load_tok.start()
    load_cot.start()
    pairs = ((w4_in, w4), (wk_in, wk), (wv_in, wv), (wg_in, wg))
    if gathers:
        gathers.begin()
    else:
        loads = [local(source, target, sems.at[2 + i]) for i, (source, target) in enumerate(pairs)]
        for copy in loads:
            copy.start()
    fill_mask(lengths, mask, length)
    load_tok.wait()
    widen(half.at[0], nat)
    if gathers:
        gathers.merge()
        gathers.vectors.step(1)

    @pl.loop(0, steps, unroll=2)
    def _(step):
        rows = take_step(nat, step, steps)
        mid[rows_at(step, SEG), :] = rows
        normed, scale = norm_rows(rows)
        norm[rows_at(step + 1, SEG), :] = normed
        rsd[0, rows_at(step, SEG), :] = jnp.broadcast_to(scale, (SEG, LANES))

    norm[0:SEG, :] = pltpu.roll(norm[length : length + SEG, :], 1, 0)
    save_n1 = local(norm, n1_out, sems.at[6])
    save_n1.start()
    if gathers:
        gathers.vectors.step(2)
        stage(1)
        gathers.vectors.step(3)
    load_cot.wait()
    widen(half.at[1], nat)
    if gathers:
        gathers.vectors.step(4)
        join_vectors(tiles, vec, share)

    @pl.loop(0, steps, unroll=2)
    def _(step):
        gain, bias = vec[0:1, :], vec[1:2, :]
        rows = rows_at(step, SEG)
        now = norm[rows_at(step + 1, SEG), :] * gain + bias
        before = (norm[rows, :] * gain + bias) * wide_of(mask[rows, :], width)
        change = now - before
        for q in range(3):
            half[2 + q, rows, :] = (before + vec[2 + q : 3 + q, :] * change).astype(BF16)

    save_mix = local(half.at[2:5], mix_out, sems.at[7])
    save_mix.start()
    stage(2)

    @pl.loop(0, steps, unroll=2)
    def _(step):
        half[0, rows_at(step, SEG), :] = take_step(nat, step, steps).astype(BF16)

    save_up = local(half.at[0], up_out, sems.at[13])
    save_up.start()
    stage(3)
    stage(4)

    if not gathers:
        for copy in loads:
            copy.wait()
    for q in (1, 2, 0):
        if q == 0:
            stage(5)

        @pl.loop(0, 2)
        def _(part):
            rows = rows_at(part, length // 2)
            pre = dot_nn(half[2 + q, rows, :], w4[:, :, :, q].reshape(width, width))
            if q == 0:
                pre = jax.nn.sigmoid(pre)
            if q == 1:
                put_rows(keys, rows, jnp.exp(pre))
            else:
                state[q // 2, rows, :] = pre

    rate = -jnp.exp(vec[5:6, :])
    fade = jnp.exp(rate)

    def first(step, carry):
        top, bottom, through = carry
        rows = rows_at(step, SEG)
        keep = mask[rows, :]
        factor = fade * wide_of(keep, width)
        key = take_rows(keys, rows)
        return factor * top + key * state[1, rows, :], factor * bottom + key, through * keep

    zero = jnp.zeros((SEG, width), F32)
    top, bottom, through = lax.fori_loop(0, steps, first, (zero, zero, jnp.ones((SEG, LANES), F32)), unroll=2)
    through = wide_of(through, width) * jnp.exp(rate * steps)
    top, bottom = join_runs((top, bottom), through, False)

    stage(6)

    def second(step, carry):
        top, bottom = carry
        rows = rows_at(step, SEG)
        keep = wide_of(mask[rows, :], width)
        top, bottom = top * keep, bottom * keep
        key = take_rows(keys, rows)
        key_value = key * state[1, rows, :]
        bonus = jnp.exp(vec[6:7, :])
        blended = (top + bonus * key_value) / (bottom + bonus * key)
        half[5, rows, :] = (state[0, rows, :] * blended).astype(BF16)
        state[2, rows, :] = top
        state[3, rows, :] = bottom
        return fade * top + key_value, fade * bottom + key

    lax.fori_loop(0, steps, second, (top, bottom), unroll=2)
    save_state = local(state, state_out, sems.at[8])
    save_state.start()
    save_key = local(keys, key_out, sems.at[18])
    save_key.start()
    save_att = local(half.at[5], att_out, sems.at[9])
    save_att.start()

    stage(7)

    @pl.loop(0, 2)
    def _(part):
        rows = rows_at(part, length // 2)
        mid[rows, :] += dot_nn(half[5, rows, :], w4[:, :, :, 3].reshape(width, width))

    stage(8)

    save_n1.wait()

    @pl.loop(0, steps, unroll=2)
    def _(step):
        rows = rows_at(step, SEG)
        normed, scale = norm_rows(mid[rows, :])
        norm[rows_at(step + 1, SEG), :] = normed
        rsd[1, rows, :] = jnp.broadcast_to(scale, (SEG, LANES))

    norm[0:SEG, :] = pltpu.roll(norm[length : length + SEG, :], 1, 0)
    save_n2 = local(norm, n2_out, sems.at[10])
    save_n2.start()
    save_r = local(rsd, r_out, sems.at[11])
    save_r.start()
    save_mix.wait()

    @pl.loop(0, steps, unroll=2)
    def _(step):
        gain, bias = vec[7:8, :], vec[8:9, :]
        rows = rows_at(step, SEG)
        now = norm[rows_at(step + 1, SEG), :] * gain + bias
        before = (norm[rows, :] * gain + bias) * wide_of(mask[rows, :], width)
        change = now - before
        for q in range(2):
            half[2 + q, rows, :] = (before + vec[9 + q : 10 + q, :] * change).astype(BF16)

    save_cig = local(half.at[2:4], cig_out, sems.at[12])
    save_cig.start()

    stage(9)

    for q in range(4):

        @pl.loop(0, 2)
        def _(part):
            rows = rows_at(part, length // 2)
            pre = jnp.maximum(dot_nn(half[2, rows, :], wk[:, :, :, q].reshape(width, width)), 0.0)
            sq[rows, q * width : (q + 1) * width] = (pre * pre).astype(BF16)

    save_sq = local(sq, sq_out, sems.at[14])
    save_sq.start()

    save_state.wait()

    @pl.loop(0, 2)
    def _(part):
        rows = rows_at(part, length // 2)
        state[0, rows, :] = jax.nn.sigmoid(dot_nn(half[3, rows, :], wg[...].reshape(width, width)))

    stage(10)
    stage(11)
    if gathers:
        saves = [
            local(source, target, sems.at[i])
            for source, target, i in (
                (w4, w4_out, 2), (wk, wk_out, 3), (wv, wv_out, 4), (wg, wg_out, 5), (vec, vec_out, 17)
            )
        ]
        for copy in saves:
            copy.start()

    @pl.loop(0, 2)
    def _(part):
        rows = rows_at(part, length // 2)
        state[1, rows, :] = dot_nn(sq[rows, :], wv[...].reshape(4 * width, width))

    save_att.wait()

    @pl.loop(0, steps, unroll=2)
    def _(step):
        rows = rows_at(step, SEG)
        gate, shrunk = state[0, rows, :], state[1, rows, :]
        upstream = half[0, rows, :].astype(F32)
        gated = gate * shrunk
        put_step(nat, step, steps, mid[rows, :] + gated)
        half[4, rows, :] = (upstream * gate).astype(BF16)
        half[5, rows, :] = (upstream * gated * (1.0 - gate)).astype(BF16)

    save_gsg = local(half.at[4:6], gsg_out, sems.at[15])
    save_gsg.start()
    narrow(nat, half.at[1])
    save_res = local(half.at[1], result, sems.at[16])
    save_res.start()
    for copy in (save_key, save_n2, save_r, save_cig, save_up, save_sq, save_gsg, save_res):
        copy.wait()
    if gathers:
        for copy in saves:
            copy.wait()
        gathers.finish()


def backward_kernel(direct, *refs):
    lengths, vec, w4_in, wk_in, wv_in, wg_in, n1_in, n2_in, r_in, mix_in, state_in, key_in = refs[:12]
    att_in, cig_in, sq_in, gsg_in, up_in, input_grad, vec_grad, g4_out, gk_out, gv_out, gg_out = refs[12:23]
    weights, big, keys, sq, half, mask, rsd, grad, grad_gate, sums, sems = refs[23:34]
    length, width = input_grad.shape
    steps = length // SEG
    n_buf, gm_buf, nb_buf, s_buf = 0, 1, 2, 3
    gate_buf, value_buf, top_buf, bottom_buf = 3, 4, 5, 6
    scatters = None
    if direct:
        total, first_y, first_x, second_in, third, s4, sk, sv, sg, a4, ak, av, ag, send, recv, free = refs[34:]
        scatters = Scatters(
            grad, grad_gate, {"4": g4_out, "k": gk_out, "v": gv_out, "g": gg_out},
            (total, first_y, first_x, second_in, third),
            {"4": s4, "k": sk, "v": sv, "g": sg}, {"4": a4, "k": ak, "v": av, "g": ag}, sums, send, recv, free,
        )

    def take(name, *steps_of):
        if scatters:
            for qs, number in steps_of:
                scatters.step(name, qs, number)

    def keep(source, target, sem):
        if not scatters:
            copy = local(source, target, sems.at[sem])
            copy.start()
            copy.wait()

    front, back = (0, 1), (2, 3)
    load_gsg = local(gsg_in, half.at[0:2], sems.at[0])
    load_sq = local(sq_in, sq, sems.at[1])
    load_wv = local(wv_in, weights, sems.at[2])
    load_cig = local(cig_in, half.at[2:4], sems.at[3])
    load_wg = local(wg_in, grad_gate, sems.at[5])
    load_n2 = local(n2_in, big.at[n_buf], sems.at[6])
    load_r2 = local(r_in.at[1], rsd, sems.at[7])
    for copy in (load_gsg, load_sq, load_wv, load_cig, load_wg, load_n2, load_r2):
        copy.start()
    if scatters:
        greet(scatters.place)
    fill_mask(lengths, mask, length)

    load_gsg.wait()
    load_sq.wait()

    @pl.loop(0, 4)
    def _(part):
        out = dot_tn(sq[:, rows_at(part, width)], half[0]).astype(BF16)
        grad[part] = out.reshape(2, 2, 4, 48, width)

    take("v", (front, 0), (back, 0))
    keep(grad, gv_out, 8)

    load_wv.wait()

    def expand_back(part):
        cols = rows_at(part, width)

        @pl.loop(0, 2)
        def _(number):
            rows = rows_at(number, length // 2)
            back_part = dot_nt(half[0, rows, :], weights[part].reshape(width, width))
            expanded = jnp.sqrt(sq[rows, cols].astype(F32))
            sq[rows, cols] = (2.0 * expanded * back_part).astype(BF16)

    pl.loop(0, 2)(expand_back)
    take("v", (front, 1))
    pl.loop(2, 4)(expand_back)
    load_wk = local(wk_in, weights, sems.at[4])
    load_wk.start()
    take("v", (back, 1))

    load_cig.wait()
    if scatters:
        for q in range(4):
            scatters.pieces["v", q].sent(0)

    def key_grad(q):
        grad[:, :, :, q] = dot_tn(half[2], sq[:, q * width : (q + 1) * width]).astype(BF16).reshape(4, 2, 2, 48, width)

    key_grad(0)
    key_grad(1)
    take("k", (front, 0))
    key_grad(2)
    key_grad(3)
    take("k", (back, 0))
    take("v", (front, 2))
    keep(grad, gk_out, 13)

    load_wg.wait()

    @pl.loop(0, 2)
    def _(part):
        rows = rows_at(part, length // 2)
        big[s_buf, rows, :] = dot_nt(half[1, rows, :], grad_gate[...].reshape(width, width))

    grad_gate[...] = dot_tn(half[3], half[1]).astype(BF16).reshape(4, 2, 2, 1, 48, width)
    take("g", ((0,), 0))
    take("k", (front, 1))
    keep(grad_gate, gg_out, 10)

    load_wk.wait()

    @pl.loop(0, 2)
    def _(part):
        rows = rows_at(part, length // 2)
        for q in range(4):
            out = dot_nt(sq[rows, q * width : (q + 1) * width], weights[:, :, :, q].reshape(width, width))
            big[gm_buf, rows, :] = out if q == 0 else big[gm_buf, rows, :] + out

    load_up = local(up_in, half.at[1], sems.at[11])
    load_up.start()
    load_w4 = local(w4_in, weights, sems.at[12])
    load_w4.start()
    load_att = local(att_in, sq.at[:, 0:width], sems.at[14])
    load_att.start()
    load_mix_key = local(mix_in.at[1:3], half.at[2:4], sems.at[9])
    load_mix_key.start()
    take("v", (back, 2))
    take("k", (back, 1))
    take("v", (front, 3))

    load_n2.wait()
    load_r2.wait()

    zero8 = jnp.zeros((8, width), F32)
    zero = jnp.zeros((SEG, width), F32)

    def fold(rows):
        return rows[0:8] + rows[8:16]

    def put_sum(row, value):
        sums[0, row : row + 1, :] = jnp.sum(value, axis=0, keepdims=True)

    def mix_two(step, carry):
        sum_channel, sum_gate = carry
        rows = rows_at(step, SEG)
        gain, bias = vec[7:8, :], vec[8:9, :]
        keep = wide_of(mask[rows, :], width)
        now = big[n_buf, rows_at(step + 1, SEG), :] * gain + bias
        before = (big[n_buf, rows, :] * gain + bias) * keep
        change = now - before
        in_channel, in_gate = big[gm_buf, rows, :], big[s_buf, rows, :]
        mix_channel, mix_gate = vec[9:10, :], vec[10:11, :]
        scaled = mix_channel * in_channel + mix_gate * in_gate
        big[gm_buf, rows, :] = scaled
        big[nb_buf, rows, :] = (in_channel + in_gate - scaled) * keep
        return sum_channel + fold(in_channel * change), sum_gate + fold(in_gate * change)

    sum_channel, sum_gate = lax.fori_loop(0, steps, mix_two, (zero8, zero8), unroll=2)
    put_sum(9, sum_channel)
    put_sum(10, sum_gate)
    big[nb_buf, length : length + SEG, :] = pltpu.roll(big[nb_buf, 0:SEG, :], SEG - 1, 0)
    load_up.wait()
    take("g", ((0,), 1))
    take("k", (front, 2))
    take("v", (back, 3))

    def norm_two(step, carry):
        sum_gain, sum_bias = carry
        rows = rows_at(step, SEG)
        normed = big[n_buf, rows_at(step + 1, SEG), :]
        incoming = big[gm_buf, rows, :] + big[nb_buf, rows_at(step + 1, SEG), :]
        scaled = incoming * vec[7:8, :]
        mean = jnp.mean(scaled, axis=-1, keepdims=True)
        along = jnp.mean(scaled * normed, axis=-1, keepdims=True)
        scale = wide_of(rsd[rows, :], width)
        out = half[1, rows, :].astype(F32) + scale * (scaled - mean - normed * along)
        big[gm_buf, rows, :] = out
        half[0, rows, :] = out.astype(BF16)
        return sum_gain + fold(incoming * normed), sum_bias + fold(incoming)

    sum_gain, sum_bias = lax.fori_loop(0, steps, norm_two, (zero8, zero8), unroll=2)
    put_sum(7, sum_gain)
    put_sum(8, sum_bias)
    load_n1 = local(n1_in, big.at[n_buf], sems.at[15])
    load_n1.start()
    load_state = local(state_in, big.at[3:7, 0:length], sems.at[16])
    load_state.start()
    load_key = local(key_in, keys, sems.at[17])
    load_key.start()
    load_r1 = local(r_in.at[0], rsd, sems.at[18])
    load_r1.start()
    load_mix = local(mix_in.at[0], half.at[1], sems.at[19])
    load_mix.start()
    if scatters:
        scatters.close("v", front)
    take("k", (back, 2))

    load_att.wait()
    load_w4.wait()
    if scatters:
        for q in range(4):
            scatters.pieces["k", q].sent(0)
    grad[:, :, :, 3] = dot_tn(sq[:, 0:width], half[0]).astype(BF16).reshape(4, 2, 2, 48, width)

    @pl.loop(0, 2)
    def _(part):
        rows = rows_at(part, length // 2)
        big[nb_buf, rows, :] = dot_nt(half[0, rows, :], weights[:, :, :, 3].reshape(width, width))

    take("g", ((0,), 2))
    take("k", (front, 3))
    if scatters:
        scatters.close("v", back)
        scatters.send_rows("v")

    rate = -jnp.exp(vec[5:6, :])
    fade = jnp.exp(rate)
    load_state.wait()
    load_key.wait()

    def first(index, carry):
        right, below, through = carry
        step = steps - 1 - index
        rows = rows_at(step, SEG)
        keep_column = mask[rows, :]
        keep = wide_of(keep_column, width)
        bonus = jnp.exp(vec[6:7, :])
        gate, key, value = big[gate_buf, rows, :], take_rows(keys, rows), big[value_buf, rows, :]
        own = bonus * key
        inverse = 1.0 / (big[bottom_buf, rows, :] + own)
        blended = (big[top_buf, rows, :] + own * value) * inverse
        incoming = big[nb_buf, rows, :] * gate
        sq[rows, width : 2 * width] = (incoming * blended * (1.0 - gate)).astype(BF16)
        weight = incoming * inverse
        big[nb_buf, rows, :] = weight
        big[gate_buf, rows, :] = blended
        right = keep * (weight + fade * right)
        below = keep * (weight * blended + fade * below)
        return right, below, through * keep_column

    right, below, through = lax.fori_loop(0, steps, first, (zero, zero, jnp.ones((SEG, LANES), F32)), unroll=2)
    through = wide_of(through, width) * jnp.exp(rate * steps)
    right, below = join_runs((right, below), through, True)
    take("k", (back, 3))
    take("g", ((0,), 3))
    if scatters:
        scatters.release()

    def second(index, carry):
        right, below, sum_decay, sum_bonus = carry
        step = steps - 1 - index
        rows = rows_at(step, SEG)
        keep = wide_of(mask[rows, :], width)
        bonus = jnp.exp(vec[6:7, :])
        weight, blended = big[nb_buf, rows, :], big[gate_buf, rows, :]
        key, value = take_rows(keys, rows), big[value_buf, rows, :]
        own = bonus * key * weight
        own_key = own * (value - blended)
        sq[rows, 2 * width : 3 * width] = (own_key + key * (right * value - below)).astype(BF16)
        sq[rows, 3 * width : 4 * width] = (own + key * right).astype(BF16)
        sum_bonus = sum_bonus + fold(own_key)
        sum_decay = sum_decay + fold(right * big[top_buf, rows, :] - below * big[bottom_buf, rows, :])
        right = keep * (weight + fade * right)
        below = keep * (weight * blended + fade * below)
        return right, below, sum_decay, sum_bonus

    _, _, sum_decay, sum_bonus = lax.fori_loop(0, steps, second, (right, below, zero8, zero8), unroll=2)
    sums[0, 5:6, :] = jnp.sum(sum_decay, axis=0, keepdims=True) * (rate * fade)
    put_sum(6, sum_bonus)

    load_mix.wait()
    load_mix_key.wait()
    if scatters:
        scatters.claim()
    for q in range(3):
        grad[:, :, :, q] = (
            dot_tn(half[1 + q], sq[:, (q + 1) * width : (q + 2) * width]).astype(BF16).reshape(4, 2, 2, 48, width)
        )
        if q == 1:
            take("4", (front, 0))
    take("4", (back, 0))
    keep(grad, g4_out, 13)
    if scatters:
        scatters.close("k", front)
    for q, place in enumerate((gate_buf, top_buf, bottom_buf)):

        @pl.loop(0, 2)
        def _(part):
            rows = rows_at(part, length // 2)
            big[place, rows, :] = dot_nt(
                sq[rows, (q + 1) * width : (q + 2) * width], weights[:, :, :, q].reshape(width, width)
            )

        if q == 0:
            take("4", (front, 1))
        if q == 1:
            take("4", (back, 1))
        if q == 2 and scatters:
            scatters.close("k", back)
            scatters.send_rows("k")

    load_n1.wait()
    load_r1.wait()

    def mix_one(step, carry):
        rows = rows_at(step, SEG)
        gain, bias = vec[0:1, :], vec[1:2, :]
        keep = wide_of(mask[rows, :], width)
        now = big[n_buf, rows_at(step + 1, SEG), :] * gain + bias
        before = (big[n_buf, rows, :] * gain + bias) * keep
        change = now - before
        out = []
        scaled, total = None, None
        for q, place in enumerate((gate_buf, top_buf, bottom_buf)):
            incoming = big[place, rows, :]
            part = vec[2 + q : 3 + q, :] * incoming
            scaled = part if scaled is None else scaled + part
            total = incoming if total is None else total + incoming
            out.append(carry[q] + fold(incoming * change))
        big[gate_buf, rows, :] = scaled
        big[nb_buf, rows, :] = (total - scaled) * keep
        return tuple(out)

    sum_mix = lax.fori_loop(0, steps, mix_one, (zero8, zero8, zero8), unroll=2)
    for q in range(3):
        put_sum(2 + q, sum_mix[q])
    big[nb_buf, length : length + SEG, :] = pltpu.roll(big[nb_buf, 0:SEG, :], SEG - 1, 0)
    if scatters:
        scatters.close("g", (0,))
        scatters.send_rows("g")
    take("4", (front, 2))

    def norm_one(step, carry):
        sum_gain, sum_bias = carry
        rows = rows_at(step, SEG)
        normed = big[n_buf, rows_at(step + 1, SEG), :]
        incoming = big[gate_buf, rows, :] + big[nb_buf, rows_at(step + 1, SEG), :]
        scaled = incoming * vec[0:1, :]
        mean = jnp.mean(scaled, axis=-1, keepdims=True)
        along = jnp.mean(scaled * normed, axis=-1, keepdims=True)
        scale = wide_of(rsd[rows, :], width)
        out = big[gm_buf, rows, :] + scale * (scaled - mean - normed * along)
        put_step(keys, step, steps, out)
        return sum_gain + fold(incoming * normed), sum_bias + fold(incoming)

    sum_gain, sum_bias = lax.fori_loop(0, steps, norm_one, (zero8, zero8), unroll=2)
    put_sum(0, sum_gain)
    put_sum(1, sum_bias)
    sums[0, 11:16, :] = jnp.zeros((5, width), F32)
    if scatters:
        scatters.hop(0)
    take("4", (back, 2))
    take("4", (front, 3))
    narrow(keys, half.at[0])
    save_in = local(half.at[0], input_grad, sems.at[20])
    save_in.start()
    if scatters:
        scatters.hop(1)
        scatters.take_rows("v")
        scatters.hop(2)
        scatters.take_rows("k")
        scatters.hop(3)
        scatters.take_rows("g")
        take("4", (back, 3))
        scatters.hop(4)
        vec_grad[...] = sums[3] + sums[7] + sums[8] + sums[9]
        scatters.close("4", front)
        scatters.close("4", back)
        scatters.send_rows("4")
        scatters.take_rows("4")
        scatters.finish()
    else:
        vec_grad[...] = sums[0]
    save_in.wait()


ANY = pl.BlockSpec(memory_space=pl.ANY)
SMEM = pl.BlockSpec(memory_space=pltpu.SMEM)
VMEM = pl.BlockSpec(memory_space=pltpu.VMEM)


def run_forward(lengths, tokens, cotangent, vec, w4, wk, wv, wg, share=None):
    length, width = tokens.shape
    shape = jax.ShapeDtypeStruct
    outs = (
        shape((length, width), BF16),
        shape((length + SEG, width), F32),
        shape((length + SEG, width), F32),
        shape((2, length, LANES), F32),
        shape((3, length, width), BF16),
        shape((4, length, width), F32),
        shape((width // LANES, length, LANES), F32),
        shape((length, width), BF16),
        shape((2, length, width), BF16),
        shape((length, 4 * width), BF16),
        shape((2, length, width), BF16),
        shape((length, width), BF16),
    )
    slabs, gate = (4, 2, 2, 4, 48, width), (4, 2, 2, 1, 48, width)
    scratch = [
        pltpu.VMEM(slabs, BF16),
        pltpu.VMEM(slabs, BF16),
        pltpu.VMEM(slabs, BF16),
        pltpu.VMEM(gate, BF16),
        pltpu.VMEM((width // LANES, length, LANES), F32),
        pltpu.VMEM((length + SEG, width), F32),
        pltpu.VMEM((length, width), F32),
        pltpu.VMEM((4, length, width), F32),
        pltpu.VMEM((width // LANES, length, LANES), F32),
        pltpu.VMEM((6, length, width), BF16),
        pltpu.VMEM((length, 4 * width), BF16),
        pltpu.VMEM((length, LANES), F32),
        pltpu.VMEM((2, length, LANES), F32),
        pltpu.SemaphoreType.DMA((19,)),
    ]
    in_specs = [SMEM, ANY, ANY, VMEM, ANY, ANY, ANY, ANY]
    params = {}
    if share:
        outs += (shape(slabs, BF16),) * 3 + (shape(gate, BF16), shape((16, width), F32))
        scratch += [pltpu.VMEM(part.shape[1:], BF16) for part in (w4, wk, wv, wg)]
        scratch += [
            pltpu.VMEM((4, 2, 2, 2, 16, LANES), F32),
            pltpu.VMEM((16, width), F32),
            pltpu.SemaphoreType.DMA((15, 6)),
            pltpu.SemaphoreType.DMA((15, 6)),
        ]
        in_specs = [SMEM, ANY, ANY, VMEM, VMEM, VMEM, VMEM, VMEM]
        params = dict(collective_id=0, has_side_effects=True)
    return pl.pallas_call(
        partial(forward_kernel, share),
        out_shape=outs,
        in_specs=in_specs,
        out_specs=[ANY] * len(outs),
        scratch_shapes=scratch,
        compiler_params=pltpu.CompilerParams(vmem_limit_bytes=VMEM_LIMIT, **params),
        name="forward",
    )(lengths, tokens, cotangent, vec, w4, wk, wv, wg)


def run_backward(lengths, vec, w4, wk, wv, wg, saved, direct):
    n1, n2, r, mix, state, keys, att, cig, sq, gsg, up = saved
    length, width = up.shape
    half = width // 2
    shape = jax.ShapeDtypeStruct
    slabs, gate = (4, 2, 2, 4, 48, width), (4, 2, 2, 1, 48, width)
    outs = (shape((length, width), BF16), shape((16, width), F32))
    out_specs = [ANY, VMEM]
    scratch = [
        pltpu.VMEM(slabs, BF16),
        pltpu.VMEM((7, length + SEG, width), F32),
        pltpu.VMEM((width // LANES, length, LANES), F32),
        pltpu.VMEM((length, 4 * width), BF16),
        pltpu.VMEM((4, length, width), BF16),
        pltpu.VMEM((length, LANES), F32),
        pltpu.VMEM((length, LANES), F32),
        pltpu.VMEM(slabs, BF16),
        pltpu.VMEM(gate, BF16),
        pltpu.VMEM((10, 16, width), F32),
        pltpu.SemaphoreType.DMA((21,)),
    ]
    params = {}
    if direct:
        rows = ((4, 24), (4, 24), (2, 48), (1, 24))
        outs += tuple(shape(part + (width,), F32) for part in rows)
        out_specs += [VMEM] * 4
        scratch += [
            pltpu.VMEM((9, 4, 2, 48, width), BF16),
            pltpu.VMEM((5, 4, 2, 48, half), BF16),
            pltpu.VMEM((4, 4, 48, width), BF16),
            pltpu.VMEM((9, 4, 48, half), BF16),
            pltpu.VMEM((9, 3, 48, half), BF16),
        ]
        scratch += [pltpu.VMEM(part + (half,), BF16) for part in rows] * 2
        scratch += [
            pltpu.SemaphoreType.DMA((15, 6)), pltpu.SemaphoreType.DMA((15, 6)), pltpu.SemaphoreType.REGULAR
        ]
        params = dict(collective_id=1, has_side_effects=True)
    else:
        outs += (shape(slabs, BF16),) * 3 + (shape(gate, BF16),)
        out_specs += [ANY] * 4
    return pl.pallas_call(
        partial(backward_kernel, direct),
        out_shape=outs,
        in_specs=[SMEM, VMEM] + [ANY] * 15,
        out_specs=out_specs,
        scratch_shapes=scratch,
        compiler_params=pltpu.CompilerParams(vmem_limit_bytes=VMEM_LIMIT, **params),
        name="backward",
    )(lengths, vec, w4, wk, wv, wg, n1, n2, r, mix, state, keys, att, cig, sq, gsg, up)


AXES = ("wide", "narrow")


def per_device(
    direct, tokens, lengths, cotangent, vectors,
    time_recept, time_key, time_value, time_output, channel_key, channel_value, channel_recept,
):
    _, length, width = tokens.shape
    slabs, gate = (4, 2, 2, 4, 48, width), (4, 2, 2, 1, 48, width)

    if direct:
        share = vectors.shape[1]

        def halves(parts, blocks, rows):
            return jnp.moveaxis(parts.reshape(blocks, rows, 2, width // 2), 2, 0)

        tile = jnp.pad(vectors.astype(F32), ((0, 5), (0, LANES - share)))
        times = jnp.stack([time_recept, time_key, time_value, time_output])
        key = jnp.swapaxes(channel_key.reshape(24, 4, width), 0, 1)
        out = run_forward(
            lengths, tokens[0], cotangent[0], tile,
            halves(times, 4, 24), halves(key, 4, 24), halves(channel_value, 2, 48), halves(channel_recept, 1, 24),
            share=share,
        )
        w4, wk, wv, wg, vec = out[12:]
    else:

        def whole(part, axis=0):
            return lax.all_gather(part, AXES, axis=axis, tiled=True)

        vec = jnp.pad(whole(vectors, 1).astype(F32), ((0, 5), (0, 0)))
        square = [whole(m).reshape(16, 48, width) for m in (time_recept, time_key, time_value, time_output)]
        w4 = jnp.stack(square, axis=1).reshape(slabs)
        wk = jnp.swapaxes(whole(channel_key).reshape(16, 48, 4, width), 1, 2).reshape(slabs)
        wv = whole(channel_value).reshape(slabs)
        wg = whole(channel_recept).reshape(gate)
        out = run_forward(lengths, tokens[0], cotangent[0], vec, w4, wk, wv, wg)
    input_grad, vec_grad, g4, gk, gv, gg = run_backward(lengths, vec, w4, wk, wv, wg, out[1:12], direct)
    if direct:
        place = lax.axis_index("wide") * 2 + lax.axis_index("narrow")
        return (
            out[0][None],
            input_grad[None],
            lax.dynamic_slice(vec_grad, (0, place * share), (vectors.shape[0], share)),
            *[g4[q].reshape(-1) for q in range(4)],
            jnp.swapaxes(gk, 0, 1).reshape(-1),
            gv.reshape(-1),
            gg.reshape(-1),
        )

    def owned(full, axis=0):
        return lax.psum_scatter(full.astype(F32), AXES, scatter_dimension=axis, tiled=True)

    return (
        out[0][None],
        input_grad[None],
        owned(vec_grad[:11], 1),
        *[owned(g4[:, :, :, q].reshape(-1)) for q in range(4)],
        owned(jnp.swapaxes(gk.reshape(16, 4, 48, width), 1, 2).reshape(-1)),
        owned(gv.reshape(-1)),
        owned(gg.reshape(-1)),
    )


def solution(mesh):
    both = P(AXES)
    rows = P(AXES, None, None)
    direct = dict(mesh.shape) == {"wide": 16, "narrow": 2}
    return jax.shard_map(
        partial(per_device, direct),
        mesh=mesh,
        in_specs=(rows, P(AXES, None), rows, P(None, AXES)) + (both,) * 7,
        out_specs=(rows, rows, P(None, AXES)) + (both,) * 7,
        check_vma=False,
    )
```

profile of v0, /device:TPU:0, one launch (start us, length us, event | category | flops | bytes accessed | tf_op | source)
XLA Modules:
  0.0 254.5 jit_solution(6102949389655932177)
XLA Ops:
  0.6 1.3 pad_convert_fusion.refs_3_
  1.9 0.8 stack.18
  2.7 0.8 stack.17
  3.6 0.8 stack.16
  4.4 0.8 stack.15
  5.2 1.0 reshape.50
  6.2 0.1 reshape.57
  6.2 0.8 maximum_bitcast_fusion
  7.0 1.0 reshape.52
  8.0 0.7 copy.43
  8.6 0.8 reshape.53
  9.4 0.6 copy.44
  10.1 120.3 %forward.1 = (bf16[1024,768]{1,0:T(8,128)(2,1)}, f32[1040,768]{1,0:T(8,128)}, f32[1040,768]{1,0:T(8,128)}, f32[2,1024,128]{2,1,0:T(8,128)}, bf16[3,1024,768]{2,1...) custom-call(s32[1,4]{1,0:T(1,128)} %refs_0_.3, ...), custom_call_target="tpu_custom_call" | custom-call | tf_op jit(solution)/shard_map/forward/pallas_call | solution.py:1132
  130.3 111.6 %backward.1 = (bf16[1024,768]{1,0:T(8,128)(2,1)}, f32[16,768]{1,0:T(8,128)}, f32[4,24,768]{2,1,0:T(8,128)}, f32[4,24,768]{2,1,0:T(8,128)}, f32[2,48,768]{2,1,0:T(8,128)}, /*index=5*/f32[1,24,768]{2,1,0:T(8,128)}) custom-call(s32[1,4]{1,0:T(1,128)} %refs_0_.3, f32[16,768]{1,0:T(8,128)} %get-tuple-element.34.refs_1_, ...), custom_call_target="tpu_custom_call" | custom-call | tf_op jit(solution)/shard_map/backward/pallas_call | solution.py:1184
  241.9 0.0 copy-start
  241.9 0.0 copy-start.1
  241.9 1.5 constant_dynamic-slice_fusion
  243.5 1.0 fusion
  244.5 0.6 reshape_squeeze.12
  245.1 0.6 reshape_squeeze.13
  245.8 0.6 reshape_squeeze.14
  246.4 0.6 reshape_squeeze.15
  247.0 1.1 copy.37
  248.1 0.8 reshape.54
  249.0 1.7 reshape.55
  250.6 1.5 reshape.56
  252.2 0.0 copy-done
  252.2 1.1 copy.47
  253.3 0.0 copy-done.1
  253.3 1.1 copy.48
  (4 shorter events, 0.0 us)
Async XLA Ops:
  241.9 10.3 %copy-start = (bf16[1024,768]{1,0:T(8,128)(2,1)S(1)}, bf16[1024,768]{1,0:T(8,128)(2,1)}, u32[]{:S(2)}) copy-start(bf16[1024,768]{1,0:T(8,128)(2,1)} %get-tuple-element.33) | copy-start | bytes 4718596
  241.9 11.4 %copy-start.1 = (bf16[1024,768]{1,0:T(8,128)(2,1)S(1)}, bf16[1024,768]{1,0:T(8,128)(2,1)}, u32[]{:S(2)}) copy-start(bf16[1024,768]{1,0:T(8,128)(2,1)} %get-tuple-element.50) | copy-start | bytes 4718596
where the time goes:
time: 255 us; the launch traced here: 254 us
  Pallas kernels  232 us (91%)
  local copies, waits for them, and re-layouts  19.9 us (8%)
    pallas_call x1, Pallas kernels, run_forward(): pl.pallas_call(partial(forward_kernel, share), out_shape=outs, in_specs=i...  120 us
    pallas_call x1, Pallas kernels, run_backward(): pl.pallas_call(partial(backward_kernel, direct), out_shape=outs, in_specs...  112 us

commit v1 on v0

v1 whole, which is shorter than its diff:
```python
from functools import partial

import jax
import jax.numpy as jnp
from jax import lax
from jax.experimental import pallas as pl
from jax.experimental.pallas import tpu as pltpu
from jax.sharding import PartitionSpec as P


SEG = 16
TAKE = 16
MIX = 4
UNROLL = 4
LANES = 128
EPS = 1e-05
F32 = jnp.float32
BF16 = jnp.bfloat16
VMEM_LIMIT = 63 * 1024 * 1024


def wide_of(column, width):
    return jnp.concatenate([column] * (width // LANES), axis=1)


def dot_nn(left, right):
    return jnp.dot(left, right, preferred_element_type=F32)


def dot_nt(left, right):
    return lax.dot_general(left, right, (((1,), (1,)), ((), ())), preferred_element_type=F32)


def dot_tn(left, right):
    return lax.dot_general(left, right, (((0,), (0,)), ((), ())), preferred_element_type=F32)


def local(source, target, sem):
    return pltpu.make_async_copy(source, target, sem)


def rows_at(index, size):
    return pl.ds(pl.multiple_of(index * size, size), size)


def rows_after(index, size):
    return pl.ds(pl.multiple_of(index * size + SEG, SEG), size)


def fold(rows):
    total = rows[0:8]
    for first in range(8, rows.shape[0], 8):
        total = total + rows[first : first + 8]
    return total


def fill_mask(lengths, mask, length):
    steps = length // SEG

    @pl.loop(0, length // 128)
    def _(block):
        row = block * 128 + lax.broadcasted_iota(jnp.int32, (128, LANES), 0)
        place = (row % SEG) * steps + row // SEG
        start = jnp.int32(0)
        fresh = place == 0
        for doc in range(lengths.shape[1] - 1):
            start = start + lengths[0, doc]
            fresh = jnp.logical_or(fresh, place == start)
        mask[rows_at(block, 128), :] = jnp.where(fresh, 0.0, 1.0)


def widen(source, target):
    @pl.loop(0, source.shape[0] // 32)
    def _(block):
        rows = rows_at(block, 32)
        for c in range(target.shape[0]):
            target[c, rows, :] = source[rows, c * LANES : (c + 1) * LANES].astype(F32)


def narrow(source, target):
    @pl.loop(0, target.shape[0] // 32)
    def _(block):
        rows = rows_at(block, 32)
        for c in range(source.shape[0]):
            target[rows, c * LANES : (c + 1) * LANES] = source[c, rows, :].astype(BF16)


def take_step(source, step, steps):
    strip = pl.ds(step, SEG, stride=steps)
    return jnp.concatenate([source[c, strip, :] for c in range(source.shape[0])], axis=1)


def put_step(target, step, steps, rows):
    strip = pl.ds(step, SEG, stride=steps)
    for c in range(target.shape[0]):
        target[c, strip, :] = rows[:, c * LANES : (c + 1) * LANES]


def take_rows(source, rows):
    return jnp.concatenate([source[c, rows, :] for c in range(source.shape[0])], axis=1)


def put_rows(target, rows, value):
    for c in range(target.shape[0]):
        target[c, rows, :] = value[:, c * LANES : (c + 1) * LANES]


def norm_rows(rows):
    centred = rows - jnp.mean(rows, axis=-1, keepdims=True)
    scale = lax.rsqrt(jnp.mean(centred * centred, axis=-1, keepdims=True) + EPS)
    return centred * scale, scale


def join_runs(local_end, through, backward):
    index = lax.broadcasted_iota(jnp.int32, local_end[0].shape, 0)
    if backward:
        index = SEG - 1 - index
    states = list(local_end)
    hop = 1
    while hop < SEG:
        turn = SEG - hop if backward else hop
        inside = index >= hop
        moved = pltpu.roll(through, turn, 0)
        states = [jnp.where(inside, s + through * pltpu.roll(s, turn, 0), s) for s in states]
        through = jnp.where(inside, through * moved, through)
        hop *= 2
    turn = SEG - 1 if backward else 1
    return [jnp.where(index >= 1, pltpu.roll(s, turn, 0), 0.0) for s in states]


FORWARD = (
    0, 100, 500, 1, 2, 101, 501, 200, 300, 400, 800, 900, 600, 700, 3, 4, 502, 201, 301, 1400, 1000, 1100, 1300,
    1200, 801, 401, 1500, 1800, 1600, 1700, 1401, 503, 1101, 1801, 901, 504, 1701, 5, 802, 601, 1702, 902, 701, 602,
    1001, 803, 1301, 804, 903, 702, 8, 1201, 904, 1302, 1501, 603, 1601, 604, 703, 1002, 6, 704, 7, 1402, 1502,
    1202, 9, 1602, 10, 1303, 11, 1102, 12, 1003, 1304, 13, 1403, 19, 1004, 1802, 16, 1404, 1203, 14, 1503, 1204, 18,
    1504, 1103, 20, 1104, 1603, 17, 1703, 1604, 1803, 21, 1704, 22, 1804, 23, 15,
)
BACKWARD = (
    0, 13, 200, 12, 100, 15, 201, 400, 14, 101, 300, 17, 401, 18, 301, 22, 202, 1100, 21, 102, 1000, 16, 1101, 20,
    900, 1001, 19, 203, 103, 402, 23, 901, 1200, 1, 2, 104, 403, 302, 1201, 1300, 24, 25, 1301, 26, 902, 404, 1102,
    27, 303, 3, 4, 204, 304, 1202, 1002, 1400, 1800, 5, 903, 800, 6, 1801, 7, 801, 1302, 1203, 8, 1103, 30, 700, 29,
    600, 802, 1003, 28, 701, 904, 1204, 601, 500, 32, 803, 33, 1004, 501, 31, 1303, 9, 602, 702, 1104, 1700, 10,
    804, 502, 1500, 1304, 703, 1900, 11, 1501, 1701, 1901, 603, 503, 1502, 604, 704, 1503, 504, 1600, 1601, 1504,
)


class Place:
    def __init__(self):
        index = lax.axis_index("wide")
        self.z, self.x, self.c = index // 4, index // 2 % 2, index % 2
        self.y = lax.axis_index("narrow")

    def at(self, z=None, x=None, c=None, y=None):
        z, x = self.z if z is None else z, self.x if x is None else x
        c, y = self.c if c is None else c, self.y if y is None else y
        return (z * 4 + x * 2 + c, y)

    def along_z(self, hop):
        return (self.z + hop) % 4

    def partners(self):
        return [self.at(z=self.along_z(hop)) for hop in (1, 2, 3)] + [
            self.at(x=1 - self.x), self.at(y=1 - self.y), self.at(c=1 - self.c)
        ]


def greet(place):
    barrier = pltpu.get_barrier_semaphore()
    for partner in place.partners():
        pl.semaphore_signal(barrier, inc=1, device_id=partner, device_id_type=pl.DeviceIdType.MESH)


def greeted(place):
    pl.semaphore_wait(pltpu.get_barrier_semaphore(), len(place.partners()))


def remote(source, target, send, recv, device):
    return pltpu.make_async_remote_copy(
        src_ref=source, dst_ref=target, send_sem=send, recv_sem=recv,
        device_id=device, device_id_type=pl.DeviceIdType.MESH,
    )


class Gather:
    def __init__(self, place, piece, half_cols, order, send, recv):
        every = slice(None)
        p, held, number = place, {"z": place.z, "x": place.x, "y": half_cols}, 0
        self.phases = []
        for axis in order + "c":
            ref = piece(held["z"], held["x"], p.c, held["y"])
            if axis == "z":
                targets = [p.at(z=p.along_z(hop)) for hop in (1, 2, 3)]
            else:
                targets = [{"x": p.at(x=1 - p.x), "y": p.at(y=1 - p.y), "c": p.at(c=1 - p.c)}[axis]]
            copies = []
            for target in targets:
                copies.append(remote(ref, ref, send.at[number], recv.at[number], target))
                number += 1
            self.phases.append(copies)
            held[axis] = every

    def step(self, phase):
        if phase:
            for copy in self.phases[phase - 1]:
                copy.wait_recv()
        if phase < len(self.phases):
            for copy in self.phases[phase]:
                copy.start()

    def finish(self):
        for copies in self.phases:
            for copy in copies:
                copy.wait_send()


def join_vectors(tiles, vec, share):
    width = vec.shape[1]
    lane = lax.broadcasted_iota(jnp.int32, (16, LANES), 1)
    blocks = [jnp.zeros((16, LANES), F32) for _ in range(width // LANES)]
    for index in range(width // share):
        z, x, c, y = index // 8, index // 4 % 2, index // 2 % 2, index % 2
        block, shift = index * share // LANES, index * share % LANES
        tile = tiles[z, x, c, y]
        tile = pltpu.roll(tile, shift, 1) if shift else tile
        if shift + share > LANES:
            blocks[block] += jnp.where(lane >= shift, tile, 0.0)
            blocks[block + 1] += jnp.where(lane < shift, tile, 0.0)
        else:
            blocks[block] += tile
    for block, tile in enumerate(blocks):
        vec[:, block * LANES : (block + 1) * LANES] = tile


class Gathers:
    WAYS = ("zxy", "zyx", "zxy", "zyx", "zyx", "yzx", "zyx", "zxy", "xzy", "zxy", "zxy", "yxz", "yzx")
    BLOCKS = {"4": (0, 4), "k": (4, 4), "g": (8, 1), "v": (9, 4)}

    def __init__(self, raw, weights, scratch, share, send, recv):
        self.place = place = Place()
        self.raw, self.weights, self.share = raw, weights, share
        self.flat, self.blocks, self.stages, self.tiles, self.vec = scratch
        tiles = self.tiles
        half = weights["4"].shape[-1] // 2
        self.cols = pl.ds(pl.multiple_of(place.y * half, half), half)
        self.halves = {}
        for i, (name, (first, count)) in enumerate(self.BLOCKS.items()):
            span = pl.ds(first, count)
            self.halves[name] = remote(
                self.blocks.at[1 - place.y, span], self.stages.at[span], send.at[0, i], recv.at[0, i],
                place.at(y=1 - place.y),
            )
        self.vectors = Gather(
            place, lambda z, x, c, y: tiles.at[z, x, c, y], place.y, "zxy", send.at[1], recv.at[1]
        )
        self.pieces, number = [self.vectors], 2
        for name, (_, count) in self.BLOCKS.items():
            for q in range(count):

                def piece(z, x, c, cols, ref=weights[name], q=q):
                    return ref.at[z, x, c, q, :, cols]

                order = self.WAYS[number - 2]
                self.pieces.append(Gather(place, piece, self.cols, order, send.at[number], recv.at[number]))
                number += 1

    def begin(self):
        place = self.place
        vectors = self.raw["vectors"]
        tile = self.tiles.at[place.z, place.x, place.c, place.y]
        tile[...] = jnp.zeros(tile.shape, F32)
        tile[0 : vectors.shape[0], 0 : self.share] = vectors[...].astype(F32)
        self.split("recept", 0)
        self.split("key", 1)
        self.split("value", 2)
        self.split("output", 3)
        greeted(place)
        half = self.blocks.shape[-1]
        for q in range(4):
            for h in range(2):
                self.blocks[h, 4 + q] = self.raw["expand"][q, :, h * half : (h + 1) * half]
        self.split("gate", 8)
        self.split("shrink", 9)

    def split(self, name, block):
        raw, flat = self.raw[name], self.flat
        rows = self.blocks.shape[2]
        across = flat.shape[0] // rows
        for part in range(raw.shape[0] // flat.shape[0]):
            flat[...] = raw[part * flat.shape[0] : (part + 1) * flat.shape[0], :].astype(F32)
            strips = [flat[pl.ds(j, rows, stride=across), :] for j in range(across)]
            for h in range(2):
                own = strips[h * across // 2 : (h + 1) * across // 2]
                self.blocks[h, block + part] = jnp.concatenate(own, axis=1).astype(BF16)

    def do(self, number, step):
        if number < 4:
            name = "4kgv"[number]
            if step:
                self.merge(name)
            else:
                self.halves[name].start()
            return
        self.pieces[number - 4].step(step)
        if number == 4 and step == 4:
            join_vectors(self.tiles, self.vec, self.share)

    def merge(self, name):
        place, y = self.place, self.place.y
        self.halves[name].wait_recv()
        slab = self.weights[name].at[place.z, place.x, place.c]
        first, count = self.BLOCKS[name]
        mine = [self.blocks[y, first + q].astype(F32) for q in range(count)]
        theirs = [self.stages[first + q].astype(F32) for q in range(count)]
        for q in range(count):
            if name == "v":
                pair = (mine if q < 2 else theirs)[q % 2 * 2 : q % 2 * 2 + 2]
                slab[(2 * y + q) % 4, :, self.cols] = jnp.concatenate(pair, axis=0).astype(BF16)
            else:
                upper, lower = jnp.where(y == 0, mine[q], theirs[q]), jnp.where(y == 0, theirs[q], mine[q])
                slab[q, :, self.cols] = jnp.concatenate([upper, lower], axis=0).astype(BF16)

    def finish(self):
        for copy in self.halves.values():
            copy.wait_send()
        for piece in self.pieces:
            piece.finish()


class Scatter:
    def __init__(self, place, cols, grad, total, arrivals, order, send, recv):
        p, (mine, other), every = place, cols, slice(None)
        self.place, self.mine, self.grad, self.total = place, mine, grad, total
        self.order, self.arrivals = order, arrivals
        self.copies = [[remote(grad.at[:, :, 1 - p.c], total, send.at[0], recv.at[0], p.at(c=1 - p.c))]]
        held, number = {"z": every, "x": every, "y": every}, 1
        for axis, ref in zip(order, arrivals):
            ways = {
                "z": [(p.along_z(hop), ref.at[hop - 1], p.at(z=p.along_z(hop))) for hop in (1, 2, 3)],
                "x": [(1 - p.x, ref, p.at(x=1 - p.x))],
                "y": [(other, ref, p.at(y=1 - p.y))],
            }[axis]
            copies = []
            for place_of, target, device in ways:
                at = {**held, axis: place_of}
                copies.append(
                    remote(total.at[at["z"], at["x"], :, at["y"]], target, send.at[number], recv.at[number], device)
                )
                number += 1
            self.copies.append(copies)
            held[axis] = {"z": p.z, "x": p.x, "y": mine}[axis]

    def sent(self, *phases):
        for phase in phases:
            for copy in self.copies[phase]:
                copy.wait_send()

    def step(self, number):
        if number:
            for copy in self.copies[number - 1]:
                copy.wait_recv()
        if number == 1:

            @pl.loop(0, 4)
            def _(z):
                for x in range(2):
                    self.total[z, x] += self.grad[z, x, self.place.c]

        if number in (2, 3):
            self.add(number - 2)
        if number < 4:
            for copy in self.copies[number]:
                copy.start()

    def add(self, index):
        p, total, ref, past = self.place, self.total, self.arrivals[index], self.order[: index + 1]
        cols = self.mine if "y" in past else slice(None)

        def rows(z):
            for x in (p.x,) if "x" in past else (0, 1):
                lead = (() if "z" in past else (z,)) + (() if "x" in past else (x,))
                if past[-1] == "z":
                    value = total[z, x, :, cols].astype(F32)
                    for hop in range(3):
                        value += ref[(hop,) + lead].astype(F32)
                    total[z, x, :, cols] = value.astype(BF16)
                else:
                    total[z, x, :, cols] += ref[lead if lead else ...]

        if "z" in past:
            rows(p.z)
        else:
            pl.loop(0, 4)(rows)

    def result(self):
        p, ref = self.place, self.arrivals[2]
        value = self.total[p.z, p.x, :, self.mine].astype(F32)
        if self.order[2] == "z":
            for hop in range(3):
                value += ref[hop].astype(F32)
        else:
            value += ref[...].astype(F32)
        return value


def arrival_shapes(order, width):
    shape, out = {"z": 4, "x": 2, "y": width}, []
    for axis in order:
        shape[axis] = width // 2 if axis == "y" else 1
        lead = tuple(n for n in (shape["z"], shape["x"]) if n > 1)
        out.append(((3,) if axis == "z" else ()) + lead + (48, shape["y"]))
    return out


class Scatters:
    SLOTS = {"v": (0, 1, 2, 3), "4": (0, 1, 2, 3), "k": (4, 5, 6, 7), "g": (8,)}
    WAYS = ("yxz", "xzy", "yxz", "yxz", "xyz", "yzx", "yxz", "xzy", "xzy")

    def __init__(self, grad, grad_gate, outs, total, arrivals, finals, arrived, sums, send, recv, free):
        self.place = place = Place()
        self.outs, self.finals, self.arrived, self.sums, self.free = outs, finals, arrived, sums, free
        half = grad.shape[-1] // 2
        mine = pl.ds(pl.multiple_of(place.y * half, half), half)
        other = pl.ds(pl.multiple_of((1 - place.y) * half, half), half)
        self.mine, self.other = mine, other
        self.pieces, number, self.claimed, self.greeted = {}, 0, False, False
        for name, slots in self.SLOTS.items():
            source = grad_gate if name == "g" else grad
            for q, slot in enumerate(slots):
                self.pieces[name, q] = Scatter(
                    place, (mine, other), source.at[:, :, :, q], total.at[slot], arrivals[3 * slot : 3 * slot + 3],
                    self.WAYS[slot], send.at[number], recv.at[number],
                )
                number += 1
        self.last = {
            name: remote(finals[name], arrived[name], send.at[number, i], recv.at[number, i], place.at(y=1 - place.y))
            for i, name in enumerate("4kvg")
        }
        number += 1
        to = [place.at(c=1 - place.c), place.at(y=1 - place.y), place.at(x=1 - place.x)]
        self.hops = [
            [remote(sums.at[i], sums.at[4 + i], send.at[number, i], recv.at[number, i], device)]
            for i, device in enumerate(to)
        ]
        self.hops.append([
            remote(sums.at[3], sums.at[6 + hop], send.at[number, 2 + hop], recv.at[number, 2 + hop],
                   place.at(z=place.along_z(hop)))
            for hop in (1, 2, 3)
        ])

    def do(self, number, step):
        if not self.greeted:
            self.greeted = True
            greeted(self.place)
        names = list(self.pieces)
        if number >= len(names):
            number -= len(names)
            if number == 0:
                self.release()
            elif number == 1:
                self.hop(step)
            else:
                name = "4kvg"[number - 2]
                self.take_rows(name) if step else self.send_rows(name)
            return
        name, q = names[number]
        if name == "4" and not self.claimed:
            self.claimed = True
            pl.semaphore_wait(self.free, 6)
        self.pieces[name, q].step(step)
        if step == 4:
            self.close(name, q)

    def put(self, name, q, half, value):
        out = self.outs[name]
        if name == "k":
            half_cols = value.shape[1]
            out[q, :, pl.ds(pl.multiple_of(half * half_cols, half_cols), half_cols)] = value
            return
        if name == "v":
            flat, first = out, q * value.shape[0]
        else:
            flat, first = out[q], 0
        strips = value.shape[1] // LANES
        across = 2 * strips
        for j in range(strips):
            rows = pl.ds(first * across + half * strips + j, value.shape[0], stride=across)
            flat[rows, :] = value[:, j * LANES : (j + 1) * LANES]

    def close(self, name, q):
        y, total = self.place.y, self.pieces[name, q].result()
        if name == "v":

            @pl.when(y == q // 2)
            def _():
                self.put(name, q % 2, y, total)

            @pl.when(y != q // 2)
            def _():
                self.finals[name][q % 2] = total.astype(BF16)
        else:
            half = total.shape[0] // 2
            upper, lower = total[:half], total[half:]
            self.put(name, q, y, jnp.where(y == 0, upper, lower))
            self.finals[name][q] = jnp.where(y == 0, lower, upper).astype(BF16)

    def send_rows(self, name):
        self.last[name].start()

    def take_rows(self, name):
        self.last[name].wait_recv()
        for q in range(self.arrived[name].shape[0]):
            self.put(name, q, 1 - self.place.y, self.arrived[name][q].astype(F32))

    def release(self):
        for q in range(4):
            self.pieces["v", q].sent(1, 2, 3)
        for partner in self.place.partners():
            pl.semaphore_signal(self.free, inc=1, device_id=partner, device_id_type=pl.DeviceIdType.MESH)

    def hop(self, number):
        if number:
            for copy in self.hops[number - 1]:
                copy.wait_recv()
        if 1 <= number <= 3:
            self.sums[number] = self.sums[number - 1] + self.sums[3 + number]
        if number < 4:
            for copy in self.hops[number]:
                copy.start()

    def finish(self):
        for (name, _), piece in self.pieces.items():
            if name == "v":
                continue
            piece.sent(1, 2, 3)
            if name != "k":
                piece.sent(0)
        for copy in self.last.values():
            copy.wait_send()
        for copies in self.hops:
            for copy in copies:
                copy.wait_send()


def forward_kernel(share, *refs):
    lengths, tokens, cotangent = refs[:3]
    length, width = tokens.shape
    steps = length // SEG
    names = ("vectors", "recept", "key", "value", "output", "expand", "shrink", "gate")
    inputs = 11 if share else 8
    result, n1_out, n2_out, r_out, mix_out, state_out, key_out, att_out, cig_out, sq_out, gsg_out, up_out = refs[
        inputs : inputs + 12
    ]
    rest = refs[inputs + 12 :]
    gathers = None
    if share:
        w4_out, wk_out, wv_out, wg_out, vec_out = rest[:5]
        rest = rest[5:]
    w4, wk, wv, wg, nat, norm, mid, state, keys, half, sq, mask, rsd, sems = rest[:14]
    if share:
        gathers = Gathers(
            dict(zip(names, refs[3:11])), {"4": w4, "k": wk, "v": wv, "g": wg}, rest[14:19], share, *rest[19:]
        )
        vec = gathers.vec
    else:
        vec = refs[3]

    load_tok = local(tokens, half.at[0], sems.at[0])
    load_cot = local(cotangent, half.at[1], sems.at[1])
    load_tok.start()
    load_cot.start()
    save_n1 = local(norm, n1_out, sems.at[6])
    save_mix = local(half.at[2:5], mix_out, sems.at[7])
    save_state = local(state, state_out, sems.at[8])
    save_att = local(half.at[5], att_out, sems.at[9])
    save_n2 = local(norm, n2_out, sems.at[10])
    save_r = local(rsd, r_out, sems.at[11])
    save_cig = local(half.at[2:4], cig_out, sems.at[12])
    save_up = local(half.at[0], up_out, sems.at[13])
    save_sq = local(sq, sq_out, sems.at[14])
    save_gsg = local(half.at[4:6], gsg_out, sems.at[15])
    save_res = local(half.at[1], result, sems.at[16])
    save_key = local(keys, key_out, sems.at[18])
    late = [save_key, save_n2, save_r, save_cig, save_up, save_sq, save_gsg, save_res]
    if gathers:
        save_w4, save_wk = local(w4, w4_out, sems.at[2]), local(wk, wk_out, sems.at[3])
        save_wv, save_wg = local(wv, wv_out, sems.at[4]), local(wg, wg_out, sems.at[5])
        save_vec = local(vec, vec_out, sems.at[17])
        late += [save_w4, save_wk, save_wv, save_wg, save_vec]
    two = length // 2
    carried = {}

    def keep(*copies):
        if gathers:
            for copy in copies:
                copy.start()

    def start():
        if gathers:
            greet(gathers.place)
        fill_mask(lengths, mask, length)
        if gathers:
            gathers.begin()
        else:
            loads = [local(one, other, sems.at[2 + i]) for i, (one, other) in enumerate(zip(refs[4:8], (w4, wk, wv, wg)))]
            for copy in loads:
                copy.start()
            for copy in loads:
                copy.wait()

    def tok():
        load_tok.wait()
        widen(half.at[0], nat)

    def first_norm():
        @pl.loop(0, steps // TAKE)
        def _(block):
            values = jnp.concatenate([take_step(nat, block * TAKE + i, steps) for i in range(TAKE)], axis=0)
            rows = rows_at(block, TAKE * SEG)
            normed, scale = norm_rows(values)
            mid[rows, :] = values
            norm[rows_after(block, TAKE * SEG), :] = normed
            rsd[0, rows, :] = jnp.broadcast_to(scale, (TAKE * SEG, LANES))

        norm[0:SEG, :] = pltpu.roll(norm[length : length + SEG, :], 1, 0)
        save_n1.start()

    def mix(gain_row, mix_row, count):
        @pl.loop(0, steps // MIX)
        def _(block):
            gain, bias = vec[gain_row : gain_row + 1, :], vec[gain_row + 1 : gain_row + 2, :]
            rows = rows_at(block, MIX * SEG)
            now = norm[rows_after(block, MIX * SEG), :] * gain + bias
            before = (norm[rows, :] * gain + bias) * wide_of(mask[rows, :], width)
            change = now - before
            for q in range(count):
                half[2 + q, rows, :] = (before + vec[mix_row + q : mix_row + q + 1, :] * change).astype(BF16)

    def first_mix():
        mix(0, 2, 3)
        save_mix.start()

    def cot():
        load_cot.wait()
        widen(half.at[1], nat)

    def upstream():
        @pl.loop(0, steps // TAKE)
        def _(block):
            values = jnp.concatenate([take_step(nat, block * TAKE + i, steps) for i in range(TAKE)], axis=0)
            half[0, rows_at(block, TAKE * SEG), :] = values.astype(BF16)

        save_up.start()

    def product(q):
        @pl.loop(0, 2)
        def _(part):
            rows = rows_at(part, two)
            pre = dot_nn(half[2 + q, rows, :], w4[:, :, :, q].reshape(width, width))
            if q == 0:
                state[0, rows, :] = jax.nn.sigmoid(pre)
            if q == 1:
                put_rows(keys, rows, jnp.exp(pre))
            if q == 2:
                state[1, rows, :] = pre

    def first_scan():
        rate = -jnp.exp(vec[5:6, :])
        fade = jnp.exp(rate)

        def first(step, carry):
            top, bottom, through = carry
            rows = rows_at(step, SEG)
            keep = mask[rows, :]
            factor = fade * wide_of(keep, width)
            key = take_rows(keys, rows)
            return factor * top + key * state[1, rows, :], factor * bottom + key, through * keep

        zero = jnp.zeros((SEG, width), F32)
        ones = jnp.ones((SEG, LANES), F32)
        top, bottom, through = lax.fori_loop(0, steps, first, (zero, zero, ones), unroll=UNROLL)
        through = wide_of(through, width) * jnp.exp(rate * steps)
        carried["sums"] = join_runs((top, bottom), through, False)
        carried["fade"] = fade

    def second_scan():
        fade = carried["fade"]

        def second(step, carry):
            top, bottom = carry
            rows = rows_at(step, SEG)
            keep = wide_of(mask[rows, :], width)
            top, bottom = top * keep, bottom * keep
            key = take_rows(keys, rows)
            key_value = key * state[1, rows, :]
            bonus = jnp.exp(vec[6:7, :])
            blended = (top + bonus * key_value) / (bottom + bonus * key)
            half[5, rows, :] = (state[0, rows, :] * blended).astype(BF16)
            state[2, rows, :] = top
            state[3, rows, :] = bottom
            return fade * top + key_value, fade * bottom + key

        lax.fori_loop(0, steps, second, tuple(carried["sums"]), unroll=UNROLL)
        save_state.start()
        save_key.start()
        save_att.start()

    def middle():
        @pl.loop(0, 2)
        def _(part):
            rows = rows_at(part, two)
            mid[rows, :] += dot_nn(half[5, rows, :], w4[:, :, :, 3].reshape(width, width))

        keep(*([save_w4, save_vec] if gathers else []))

    def second_norm():
        save_n1.wait()

        @pl.loop(0, steps // TAKE)
        def _(block):
            rows = rows_at(block, TAKE * SEG)
            normed, scale = norm_rows(mid[rows, :])
            norm[rows_after(block, TAKE * SEG), :] = normed
            rsd[1, rows, :] = jnp.broadcast_to(scale, (TAKE * SEG, LANES))

        norm[0:SEG, :] = pltpu.roll(norm[length : length + SEG, :], 1, 0)
        save_n2.start()
        save_r.start()

    def second_mix():
        save_mix.wait()
        mix(7, 9, 2)
        save_cig.start()

    def expanded(q):
        @pl.loop(0, 2)
        def _(part):
            rows = rows_at(part, two)
            pre = jnp.maximum(dot_nn(half[2, rows, :], wk[:, :, :, q].reshape(width, width)), 0.0)
            sq[rows, q * width : (q + 1) * width] = (pre * pre).astype(BF16)

        carried["blocks"] = carried.get("blocks", 0) + 1
        if carried["blocks"] == 4:
            save_sq.start()
            keep(*([save_wk] if gathers else []))

    def gate():
        save_state.wait()

        @pl.loop(0, 2)
        def _(part):
            rows = rows_at(part, two)
            state[0, rows, :] = jax.nn.sigmoid(dot_nn(half[3, rows, :], wg[...].reshape(width, width)))

        keep(*([save_wg] if gathers else []))

    def shrunk(q):
        @pl.loop(0, 2)
        def _(part):
            rows = rows_at(part, two)
            out = dot_nn(sq[rows, q * width : (q + 1) * width], wv[:, :, :, q].reshape(width, width))
            state[1, rows, :] = state[1, rows, :] + out if q else out

    def final():
        keep(*([save_wv] if gathers else []))
        save_att.wait()

        @pl.loop(0, steps // TAKE)
        def _(block):
            rows = rows_at(block, TAKE * SEG)
            gate_value, shrunk_value = state[0, rows, :], state[1, rows, :]
            incoming = half[0, rows, :].astype(F32)
            gated = gate_value * shrunk_value
            out = mid[rows, :] + gated
            for i in range(TAKE):
                put_step(nat, block * TAKE + i, steps, out[i * SEG : (i + 1) * SEG])
            half[4, rows, :] = (incoming * gate_value).astype(BF16)
            half[5, rows, :] = (incoming * gated * (1.0 - gate_value)).astype(BF16)

        save_gsg.start()
        narrow(nat, half.at[1])
        save_res.start()

    work = [
        start, tok, first_norm, cot, upstream, first_mix, partial(product, 0), partial(product, 1), partial(product, 2),
        first_scan, second_scan, middle, second_norm, second_mix, gate, final,
    ]
    work += [partial(expanded, q) for q in range(4)] + [partial(shrunk, q) for q in range(4)]
    for item in FORWARD:
        if item < 100:
            work[item]()
        elif gathers:
            gathers.do(item // 100 - 1, item % 100)
    for copy in late:
        copy.wait()
    if gathers:
        gathers.finish()


def backward_kernel(direct, *refs):
    lengths, vec, w4_in, wk_in, wv_in, wg_in, n1_in, n2_in, r_in, mix_in, state_in, key_in = refs[:12]
    att_in, cig_in, sq_in, gsg_in, up_in, input_grad, vec_grad = refs[12:19]
    g4_out, gk_out, gv_out, gg_out = (refs[19:23], *refs[23:26]) if direct else refs[19:23]
    rest = refs[26:] if direct else refs[23:]
    weights, big, keys, sq, half, mask, rsd, grad, grad_gate, sums, sems = rest[:11]
    rest = rest[11:]
    length, width = input_grad.shape
    steps = length // SEG
    n_buf, gm_buf, nb_buf, s_buf = 0, 1, 2, 3
    gate_buf, value_buf, top_buf, bottom_buf = 3, 4, 5, 6
    scatters = None
    if direct:
        total, arrivals, rest = rest[0], rest[1:28], rest[28:]
        scatters = Scatters(
            grad, grad_gate, {"4": g4_out, "k": gk_out, "v": gv_out, "g": [gg_out]}, total, arrivals,
            dict(zip("4kvg", rest[:4])), dict(zip("4kvg", rest[4:8])), sums, *rest[8:],
        )

    def keep(source, target, *q):
        if not scatters:
            place = (slice(None),) * 3 + q
            copy = local(source.at[place], target.at[place], sems.at[8])
            copy.start()
            copy.wait()

    load_gsg = local(gsg_in, half.at[0:2], sems.at[0])
    load_sq = [
        local(sq_in.at[:, q * width : (q + 1) * width], sq.at[:, q * width : (q + 1) * width], sems.at[19 + q])
        for q in range(4)
    ]
    load_wv = local(wv_in, weights, sems.at[2])
    load_cig = local(cig_in, half.at[2:4], sems.at[3])
    load_wk = local(wk_in, weights, sems.at[4])
    load_wg = local(wg_in, grad_gate, sems.at[5])
    load_n2 = local(n2_in, big.at[n_buf], sems.at[6])
    load_r2 = local(r_in.at[1], rsd, sems.at[7])
    load_up = local(up_in, half.at[0], sems.at[9])
    load_w4 = local(w4_in, weights, sems.at[10])
    load_att = local(att_in, sq.at[:, 0:width], sems.at[11])
    load_n1 = local(n1_in, big.at[n_buf], sems.at[12])
    load_gate = local(state_in.at[0], big.at[gate_buf, 0:length], sems.at[13])
    load_state = local(state_in.at[1:4], big.at[value_buf : bottom_buf + 1, 0:length], sems.at[14])
    load_key = local(key_in, keys, sems.at[15])
    load_r1 = local(r_in.at[0], rsd, sems.at[16])
    load_mix = local(mix_in, half.at[1:4], sems.at[17])
    save_in = local(half.at[0], input_grad, sems.at[18])
    for copy in (load_gsg, *[load_sq[q] for q in (1, 0, 3, 2)], load_wv, load_cig, load_wg, load_n2, load_r2, load_state, load_key):
        copy.start()
    two = length // 2
    zero8 = jnp.zeros((8, width), F32)
    zero = jnp.zeros((SEG, width), F32)
    carried = {}

    def put_sum(row, value):
        sums[0, row : row + 1, :] = jnp.sum(value, axis=0, keepdims=True)

    def columns(block):
        return slice(block * width, (block + 1) * width)

    def slabs(product):
        return product.astype(BF16).reshape(4, 2, 2, 48, width)

    def start():
        if scatters:
            greet(scatters.place)
        fill_mask(lengths, mask, length)
        load_gsg.wait()

    def value_grad(q):
        load_sq[q].wait()
        grad[:, :, :, q] = slabs(dot_tn(sq[:, columns(q)], half[0]))
        keep(grad, gv_out, q)

    def expand_back(q):
        if "wv" not in carried:
            carried["wv"] = 0
            load_wv.wait()
        carried["wv"] += 1

        @pl.loop(0, 2)
        def _(part):
            rows = rows_at(part, two)
            back = dot_nt(half[0, rows, :], weights[:, :, :, q].reshape(width, width))
            expanded = jnp.sqrt(sq[rows, columns(q)].astype(F32))
            sq[rows, columns(q)] = (2.0 * expanded * back).astype(BF16)

        if carried["wv"] == 4:
            load_wk.start()
            load_up.start()

    def wait_channel():
        if "cig" not in carried:
            carried["cig"] = True
            load_cig.wait()

    def key_grad(q):
        wait_channel()
        if scatters:
            scatters.pieces["v", q].sent(0)
        grad[:, :, :, q] = slabs(dot_tn(half[2], sq[:, columns(q)]))
        keep(grad, gk_out, q)

    def gate_in():
        load_wg.wait()

        @pl.loop(0, 2)
        def _(part):
            rows = rows_at(part, two)
            big[s_buf, rows, :] = dot_nt(half[1, rows, :], grad_gate[...].reshape(width, width))

    def gate_grad():
        wait_channel()
        grad_gate[...] = slabs(dot_tn(half[3], half[1])).reshape(grad_gate.shape)
        keep(grad_gate, gg_out)

    def channel_in(q):
        if q == 0:
            load_wk.wait()

        @pl.loop(0, 2)
        def _(part):
            rows = rows_at(part, two)
            out = dot_nt(sq[rows, columns(q)], weights[:, :, :, q].reshape(width, width))
            big[gm_buf, rows, :] = out if q == 0 else big[gm_buf, rows, :] + out

        if q == 3:
            load_w4.start()

    def second_mix():
        load_n2.wait()
        load_r2.wait()

        def mix_two(block, carry):
            sum_channel, sum_gate = carry
            rows, after = rows_at(block, MIX * SEG), rows_after(block, MIX * SEG)
            gain, bias = vec[7:8, :], vec[8:9, :]
            keep = wide_of(mask[rows, :], width)
            now = big[n_buf, after, :] * gain + bias
            before = (big[n_buf, rows, :] * gain + bias) * keep
            change = now - before
            in_channel, in_gate = big[gm_buf, rows, :], big[s_buf, rows, :]
            mix_channel, mix_gate = vec[9:10, :], vec[10:11, :]
            scaled = mix_channel * in_channel + mix_gate * in_gate
            big[gm_buf, rows, :] = scaled
            big[nb_buf, rows, :] = (in_channel + in_gate - scaled) * keep
            return sum_channel + fold(in_channel * change), sum_gate + fold(in_gate * change)

        sum_channel, sum_gate = lax.fori_loop(0, steps // MIX, mix_two, (zero8, zero8))
        load_gate.start()
        load_att.start()
        put_sum(9, sum_channel)
        put_sum(10, sum_gate)
        big[nb_buf, length : length + SEG, :] = pltpu.roll(big[nb_buf, 0:SEG, :], SEG - 1, 0)

    def second_norm():
        load_up.wait()

        def norm_two(block, carry):
            sum_gain, sum_bias = carry
            rows, after = rows_at(block, TAKE * SEG), rows_after(block, TAKE * SEG)
            normed = big[n_buf, after, :]
            incoming = big[gm_buf, rows, :] + big[nb_buf, after, :]
            scaled = incoming * vec[7:8, :]
            mean = jnp.mean(scaled, axis=-1, keepdims=True)
            along = jnp.mean(scaled * normed, axis=-1, keepdims=True)
            scale = wide_of(rsd[rows, :], width)
            out = half[0, rows, :].astype(F32) + scale * (scaled - mean - normed * along)
            big[gm_buf, rows, :] = out
            half[0, rows, :] = out.astype(BF16)
            return sum_gain + fold(incoming * normed), sum_bias + fold(incoming)

        sum_gain, sum_bias = lax.fori_loop(0, steps // TAKE, norm_two, (zero8, zero8))
        put_sum(7, sum_gain)
        put_sum(8, sum_bias)
        load_n1.start()
        load_r1.start()

    def output_grad():
        if scatters:
            scatters.pieces["k", 3].sent(0)
        load_att.wait()
        grad[:, :, :, 3] = slabs(dot_tn(sq[:, columns(0)], half[0]))
        keep(grad, g4_out, 3)

    def attended_back():
        load_w4.wait()

        @pl.loop(0, 2)
        def _(part):
            rows = rows_at(part, two)
            big[nb_buf, rows, :] = dot_nt(half[0, rows, :], weights[:, :, :, 3].reshape(width, width))

    def first_scan():
        load_mix.start()
        rate = -jnp.exp(vec[5:6, :])
        fade = jnp.exp(rate)
        load_gate.wait()
        load_state.wait()
        load_key.wait()

        def first(index, carry):
            right, below, through = carry
            step = steps - 1 - index
            rows = rows_at(step, SEG)
            keep_column = mask[rows, :]
            keep = wide_of(keep_column, width)
            bonus = jnp.exp(vec[6:7, :])
            gate, key, value = big[gate_buf, rows, :], take_rows(keys, rows), big[value_buf, rows, :]
            own = bonus * key
            inverse = 1.0 / (big[bottom_buf, rows, :] + own)
            blended = (big[top_buf, rows, :] + own * value) * inverse
            incoming = big[nb_buf, rows, :] * gate
            sq[rows, width : 2 * width] = (incoming * blended * (1.0 - gate)).astype(BF16)
            weight = incoming * inverse
            big[nb_buf, rows, :] = weight
            big[gate_buf, rows, :] = blended
            right = keep * (weight + fade * right)
            below = keep * (weight * blended + fade * below)
            return right, below, through * keep_column

        ones = jnp.ones((SEG, LANES), F32)
        right, below, through = lax.fori_loop(0, steps, first, (zero, zero, ones), unroll=UNROLL)
        through = wide_of(through, width) * jnp.exp(rate * steps)
        carried["sums"] = join_runs((right, below), through, True)
        carried["rate"], carried["fade"] = rate, fade

    def second_scan():
        rate, fade = carried["rate"], carried["fade"]

        def second(index, carry):
            right, below, sum_decay, sum_bonus = carry
            step = steps - 1 - index
            rows = rows_at(step, SEG)
            keep = wide_of(mask[rows, :], width)
            bonus = jnp.exp(vec[6:7, :])
            weight, blended = big[nb_buf, rows, :], big[gate_buf, rows, :]
            key, value = take_rows(keys, rows), big[value_buf, rows, :]
            own = bonus * key * weight
            own_key = own * (value - blended)
            sq[rows, 2 * width : 3 * width] = (own_key + key * (right * value - below)).astype(BF16)
            sq[rows, 3 * width : 4 * width] = (own + key * right).astype(BF16)
            sum_bonus = sum_bonus + fold(own_key)
            sum_decay = sum_decay + fold(right * big[top_buf, rows, :] - below * big[bottom_buf, rows, :])
            right = keep * (weight + fade * right)
            below = keep * (weight * blended + fade * below)
            return right, below, sum_decay, sum_bonus

        carry = (*carried["sums"], zero8, zero8)
        _, _, sum_decay, sum_bonus = lax.fori_loop(0, steps, second, carry, unroll=UNROLL)
        sums[0, 5:6, :] = jnp.sum(sum_decay, axis=0, keepdims=True) * (rate * fade)
        put_sum(6, sum_bonus)

    def time_grad(q):
        if "mix" not in carried:
            carried["mix"] = True
            load_mix.wait()
        if scatters:
            scatters.pieces["k", q].sent(0)
        grad[:, :, :, q] = slabs(dot_tn(half[1 + q], sq[:, columns(1 + q)]))
        keep(grad, g4_out, q)

    mixed_bufs = (gate_buf, top_buf, bottom_buf)

    def time_back(q):
        @pl.loop(0, 2)
        def _(part):
            rows = rows_at(part, two)
            big[mixed_bufs[q], rows, :] = dot_nt(sq[rows, columns(1 + q)], weights[:, :, :, q].reshape(width, width))

    def first_mix():
        load_n1.wait()
        load_r1.wait()

        def mix_one(block, carry):
            rows, after = rows_at(block, MIX * SEG), rows_after(block, MIX * SEG)
            gain, bias = vec[0:1, :], vec[1:2, :]
            keep = wide_of(mask[rows, :], width)
            now = big[n_buf, after, :] * gain + bias
            before = (big[n_buf, rows, :] * gain + bias) * keep
            change = now - before
            out = []
            scaled, total = None, None
            for q, place in enumerate(mixed_bufs):
                incoming = big[place, rows, :]
                part = vec[2 + q : 3 + q, :] * incoming
                scaled = part if scaled is None else scaled + part
                total = incoming if total is None else total + incoming
                out.append(carry[q] + fold(incoming * change))
            big[gate_buf, rows, :] = scaled
            big[nb_buf, rows, :] = (total - scaled) * keep
            return tuple(out)

        sum_mix = lax.fori_loop(0, steps // MIX, mix_one, (zero8, zero8, zero8))
        for q in range(3):
            put_sum(2 + q, sum_mix[q])
        big[nb_buf, length : length + SEG, :] = pltpu.roll(big[nb_buf, 0:SEG, :], SEG - 1, 0)

    def first_norm():
        def norm_one(block, carry):
            sum_gain, sum_bias = carry
            rows, after = rows_at(block, TAKE * SEG), rows_after(block, TAKE * SEG)
            normed = big[n_buf, after, :]
            incoming = big[gate_buf, rows, :] + big[nb_buf, after, :]
            scaled = incoming * vec[0:1, :]
            mean = jnp.mean(scaled, axis=-1, keepdims=True)
            along = jnp.mean(scaled * normed, axis=-1, keepdims=True)
            scale = wide_of(rsd[rows, :], width)
            out = big[gm_buf, rows, :] + scale * (scaled - mean - normed * along)
            for i in range(TAKE):
                put_step(keys, block * TAKE + i, steps, out[i * SEG : (i + 1) * SEG])
            return sum_gain + fold(incoming * normed), sum_bias + fold(incoming)

        sum_gain, sum_bias = lax.fori_loop(0, steps // TAKE, norm_one, (zero8, zero8))
        put_sum(0, sum_gain)
        put_sum(1, sum_bias)
        sums[0, 11:16, :] = jnp.zeros((5, width), F32)

    def final():
        narrow(keys, half.at[0])
        save_in.start()

    work = [
        start, gate_in, gate_grad, second_mix, second_norm, output_grad, attended_back, first_scan, second_scan, first_mix,
        first_norm, final,
    ]
    for function, count in (
        (value_grad, 4), (expand_back, 4), (key_grad, 4), (channel_in, 4), (time_grad, 3), (time_back, 3)
    ):
        work += [partial(function, q) for q in range(count)]
    for item in BACKWARD:
        if item < 100:
            work[item]()
        elif scatters:
            scatters.do(item // 100 - 1, item % 100)
    if scatters:
        vec_grad[...] = sums[3] + sums[7] + sums[8] + sums[9]
        scatters.finish()
    else:
        vec_grad[...] = sums[0]
    save_in.wait()


ANY = pl.BlockSpec(memory_space=pl.ANY)
SMEM = pl.BlockSpec(memory_space=pltpu.SMEM)
VMEM = pl.BlockSpec(memory_space=pltpu.VMEM)


def run_forward(lengths, tokens, cotangent, parameters, share=None):
    length, width = tokens.shape
    shape = jax.ShapeDtypeStruct
    outs = (
        shape((length, width), BF16),
        shape((length + SEG, width), F32),
        shape((length + SEG, width), F32),
        shape((2, length, LANES), F32),
        shape((3, length, width), BF16),
        shape((4, length, width), F32),
        shape((width // LANES, length, LANES), F32),
        shape((length, width), BF16),
        shape((2, length, width), BF16),
        shape((length, 4 * width), BF16),
        shape((2, length, width), BF16),
        shape((length, width), BF16),
    )
    slabs, gate = (4, 2, 2, 4, 48, width), (4, 2, 2, 1, 48, width)
    scratch = [
        pltpu.VMEM(slabs, BF16),
        pltpu.VMEM(slabs, BF16),
        pltpu.VMEM(slabs, BF16),
        pltpu.VMEM(gate, BF16),
        pltpu.VMEM((width // LANES, length, LANES), F32),
        pltpu.VMEM((length + SEG, width), F32),
        pltpu.VMEM((length, width), F32),
        pltpu.VMEM((4, length, width), F32),
        pltpu.VMEM((width // LANES, length, LANES), F32),
        pltpu.VMEM((6, length, width), BF16),
        pltpu.VMEM((length, 4 * width), BF16),
        pltpu.VMEM((length, LANES), F32),
        pltpu.VMEM((2, length, LANES), F32),
        pltpu.SemaphoreType.DMA((19,)),
    ]
    in_specs = [SMEM, ANY, ANY, VMEM, ANY, ANY, ANY, ANY]
    params = {}
    if share:
        outs += (shape(slabs, BF16),) * 3 + (shape(gate, BF16), shape((16, width), F32))
        scratch += [
            pltpu.VMEM((24 * width // LANES, LANES), F32),
            pltpu.VMEM((2, 13, 24, width // 2), BF16),
            pltpu.VMEM((13, 24, width // 2), BF16),
            pltpu.VMEM((4, 2, 2, 2, 16, LANES), F32),
            pltpu.VMEM((16, width), F32),
            pltpu.SemaphoreType.DMA((15, 6)),
            pltpu.SemaphoreType.DMA((15, 6)),
        ]
        in_specs = [SMEM, ANY, ANY] + [VMEM] * 8
        params = dict(collective_id=0, has_side_effects=True)
    return pl.pallas_call(
        partial(forward_kernel, share),
        out_shape=outs,
        in_specs=in_specs,
        out_specs=[ANY] * len(outs),
        scratch_shapes=scratch,
        compiler_params=pltpu.CompilerParams(vmem_limit_bytes=VMEM_LIMIT, **params),
        name="forward",
    )(lengths, tokens, cotangent, *parameters)


def run_backward(lengths, vec, w4, wk, wv, wg, saved, direct):
    n1, n2, r, mix, state, keys, att, cig, sq, gsg, up = saved
    length, width = up.shape
    half = width // 2
    shape = jax.ShapeDtypeStruct
    slabs, gate = (4, 2, 2, 4, 48, width), (4, 2, 2, 1, 48, width)
    outs = (shape((length, width), BF16), shape((16, width), F32))
    out_specs = [ANY, VMEM]
    scratch = [
        pltpu.VMEM(slabs, BF16),
        pltpu.VMEM((7, length + SEG, width), F32),
        pltpu.VMEM((width // LANES, length, LANES), F32),
        pltpu.VMEM((length, 4 * width), BF16),
        pltpu.VMEM((4, length, width), BF16),
        pltpu.VMEM((length, LANES), F32),
        pltpu.VMEM((length, LANES), F32),
        pltpu.VMEM(slabs, BF16),
        pltpu.VMEM(gate, BF16),
        pltpu.VMEM((10, 16, width), F32),
        pltpu.SemaphoreType.DMA((23,)),
    ]
    params = {}
    if direct:
        rows = ((4, 24), (4, 24), (2, 48), (1, 24))
        lines = 24 * width // LANES
        outs += (shape((lines, LANES), F32),) * 4 + (
            shape((4, 24, width), F32), shape((4 * lines, LANES), F32), shape((lines, LANES), F32)
        )
        out_specs += [VMEM] * 7
        scratch += [pltpu.VMEM((9, 4, 2, 48, width), BF16)]
        scratch += [pltpu.VMEM(part, BF16) for way in Scatters.WAYS for part in arrival_shapes(way, width)]
        scratch += [pltpu.VMEM(part + (half,), BF16) for part in rows] * 2
        scratch += [
            pltpu.SemaphoreType.DMA((15, 6)), pltpu.SemaphoreType.DMA((15, 6)), pltpu.SemaphoreType.REGULAR
        ]
        params = dict(collective_id=1, has_side_effects=True)
    else:
        outs += (shape(slabs, BF16),) * 3 + (shape(gate, BF16),)
        out_specs += [ANY] * 4
    return pl.pallas_call(
        partial(backward_kernel, direct),
        out_shape=outs,
        in_specs=[SMEM, VMEM] + [ANY] * 15,
        out_specs=out_specs,
        scratch_shapes=scratch,
        compiler_params=pltpu.CompilerParams(vmem_limit_bytes=VMEM_LIMIT, **params),
        name="backward",
    )(lengths, vec, w4, wk, wv, wg, n1, n2, r, mix, state, keys, att, cig, sq, gsg, up)


AXES = ("wide", "narrow")


def per_device(
    direct, tokens, lengths, cotangent, vectors,
    time_recept, time_key, time_value, time_output, channel_key, channel_value, channel_recept,
):
    _, length, width = tokens.shape
    slabs, gate = (4, 2, 2, 4, 48, width), (4, 2, 2, 1, 48, width)

    if direct:
        share = vectors.shape[1]
        key = channel_key.reshape(24, 16, 4, 48).transpose(2, 0, 1, 3).reshape(4, 24, width)
        flat = [m.reshape(-1, LANES) for m in (time_recept, time_key, time_value, time_output, channel_value, channel_recept)]
        out = run_forward(
            lengths, tokens[0], cotangent[0], (vectors, *flat[:4], key, flat[4], flat[5]), share=share
        )
        w4, wk, wv, wg, vec = out[12:]
    else:

        def whole(part, axis=0):
            return lax.all_gather(part, AXES, axis=axis, tiled=True)

        vec = jnp.pad(whole(vectors, 1).astype(F32), ((0, 5), (0, 0)))
        square = [whole(m).reshape(16, 48, width) for m in (time_recept, time_key, time_value, time_output)]
        w4 = jnp.stack(square, axis=1).reshape(slabs)
        wk = whole(channel_key).reshape(16, 48, 16, 4, 48).transpose(0, 3, 1, 2, 4).reshape(slabs)
        wv = whole(channel_value).reshape(slabs)
        wg = whole(channel_recept).reshape(gate)
        out = run_forward(lengths, tokens[0], cotangent[0], (vec, w4, wk, wv, wg))
    input_grad, vec_grad, *grads = run_backward(lengths, vec, w4, wk, wv, wg, out[1:12], direct)
    if direct:
        place = lax.axis_index("wide") * 2 + lax.axis_index("narrow")
        gk, gv, gg = grads[4:]
        return (
            out[0][None],
            input_grad[None],
            lax.dynamic_slice(vec_grad, (0, place * share), (vectors.shape[0], share)),
            *[g.reshape(-1) for g in grads[:4]],
            gk.reshape(4, 24, 16, 48).transpose(1, 2, 0, 3).reshape(-1),
            gv.reshape(-1),
            gg.reshape(-1),
        )
    g4, gk, gv, gg = grads

    def owned(full, axis=0):
        return lax.psum_scatter(full.astype(F32), AXES, scatter_dimension=axis, tiled=True)

    return (
        out[0][None],
        input_grad[None],
        owned(vec_grad[:11], 1),
        *[owned(g4[:, :, :, q].reshape(-1)) for q in range(4)],
        owned(gk.reshape(16, 4, 48, 16, 48).transpose(0, 2, 3, 1, 4).reshape(-1)),
        owned(gv.reshape(-1)),
        owned(gg.reshape(-1)),
    )


def solution(mesh):
    both = P(AXES)
    rows = P(AXES, None, None)
    direct = dict(mesh.shape) == {"wide": 16, "narrow": 2}
    return jax.shard_map(
        partial(per_device, direct),
        mesh=mesh,
        in_specs=(rows, P(AXES, None), rows, P(None, AXES)) + (both,) * 7,
        out_specs=(rows, rows, P(None, AXES)) + (both,) * 7,
        check_vma=False,
    )
```

time: 255 us -> 226 us (0.89)
  Pallas kernels: 232 us -> 208 us
  local copies, waits for them, and re-layouts: 19.9 us -> 14.1 us
    pallas_call x1, Pallas kernels: 120 us -> 97.1 us  [run_forward(): pl.pallas_call(partial(forward_kernel, share), out_shape=outs, in_specs=i...]
    another operation x12 -> x0, local copies, waits for them, and re-layouts: 5.77 us -> none  [the longest x8 3.22 us: per_device(): times = jnp.stack([time_recept, time_key, time_value, time_output])]
    unnamed x6 -> x24, local copies, waits for them, and re-layouts: 2.29 us -> 7.02 us
    reshape x9 -> x5, local copies, waits for them, and re-layouts: 8.16 us -> 5.49 us  [the longest x3 3.2 us: per_device(): gk.reshape(4, 24, 16, 48).transpose(1, 2, 0, 3).reshape(-1)]
where the time goes in v1:
time: 226 us; the launch traced here: 223 us
  Pallas kernels  208 us (92%)
  local copies, waits for them, and re-layouts  14.1 us (6%)
    pallas_call x1, Pallas kernels, run_backward(): pl.pallas_call(partial(backward_kernel, direct), out_shape=outs, in_specs...  111 us
    pallas_call x1, Pallas kernels, run_forward(): pl.pallas_call(partial(forward_kernel, share), out_shape=outs, in_specs=i...  97.1 us
    unnamed x24, local copies, waits for them, and re-layouts  7.02 us

profile of v1, /device:TPU:0, one launch (start us, length us, event | category | flops | bytes accessed | tf_op | source)
XLA Modules:
  0.0 223.3 jit_solution(5906216581266795187)
XLA Ops:
  0.6 1.3 reshape.72
  1.9 0.1 copy.21
  2.0 1.0 reshape.73.refs_8_
  3.0 97.1 %forward.1 = (bf16[1024,768]{1,0:T(8,128)(2,1)}, f32[1040,768]{1,0:T(8,128)}, f32[1040,768]{1,0:T(8,128)}, f32[2,1024,128]{2,1,0:T(8,128)}, bf16[3,1024,768]{2,1...) custom-call(s32[1,4]{1,0:T(1,128)} %refs_0_.3, ...), custom_call_target="tpu_custom_call" | custom-call | tf_op jit(solution)/shard_map/forward/pallas_call | solution.py:1196
  100.1 111.2 %backward.1 = (bf16[1024,768]{1,0:T(8,128)(2,1)}, f32[16,768]{1,0:T(8,128)}, f32[144,128]{1,0:T(8,128)}, f32[144,128]{1,0:T(8,128)}, f32[144,128]{1,0:T(8,128)},...) custom-call(s32[1,4]{1,0:T(1,128)} %refs_0_.3, ...), custom_call_target="tpu_custom_call" | custom-call | tf_op jit(solution)/shard_map/backward/pallas_call | solution.py:1246
  211.3 0.0 copy-start
  211.3 1.5 constant_dynamic-slice_fusion
  212.8 1.4 reshape.80
  214.2 0.5 copy.24
  214.7 1.3 reshape.81
  216.0 0.0 copy-start.1
  216.0 0.0 copy-done
  216.0 0.0 copy-start.7
  216.0 0.0 copy-start.5
  216.1 0.0 copy-start.4
  216.1 0.0 copy-start.2
  216.1 0.0 copy-start.3
  216.1 1.1 copy.33
  217.2 0.8 copy-done.1
  218.0 1.1 copy.34
  219.1 0.0 copy-done.7
  219.2 0.6 copy.35
  219.8 0.0 copy-done.6
  219.8 0.6 copy.36
  220.4 0.0 copy-done.5
  220.4 0.6 copy.37
  221.1 0.0 copy-done.4
  221.1 0.6 copy.38
  221.7 0.0 copy-done.2
  221.7 0.7 copy.39
  222.4 0.0 copy-done.3
  222.5 0.6 copy.40
  (1 shorter events, 0.0 us)
Async XLA Ops:
  211.3 4.8 %copy-start = (bf16[1024,768]{1,0:T(8,128)(2,1)S(1)}, bf16[1024,768]{1,0:T(8,128)(2,1)}, u32[]{:S(2)}) copy-start(bf16[1024,768]{1,0:T(8,128)(2,1)} %get-tuple-element.36) | copy-start | bytes 4718596
  216.0 2.0 copy-start.1
  216.0 3.1 %copy-start.7 = (f32[144,128]{1,0:T(8,128)S(1)}, f32[144,128]{1,0:T(8,128)}, u32[]{:S(2)}) copy-start(f32[144,128]{1,0:T(8,128)} %get-tuple-element.55) | copy-start | bytes 221188
  216.0 3.8 %copy-start.6 = (f32[144,128]{1,0:T(8,128)S(1)}, f32[144,128]{1,0:T(8,128)}, u32[]{:S(2)}) copy-start(f32[144,128]{1,0:T(8,128)} %get-tuple-element.56) | copy-start | bytes 221188
  216.0 4.4 %copy-start.5 = (f32[144,128]{1,0:T(8,128)S(1)}, f32[144,128]{1,0:T(8,128)}, u32[]{:S(2)}) copy-start(f32[144,128]{1,0:T(8,128)} %get-tuple-element.57) | copy-start | bytes 221188
  216.1 5.0 %copy-start.4 = (f32[144,128]{1,0:T(8,128)S(1)}, f32[144,128]{1,0:T(8,128)}, u32[]{:S(2)}) copy-start(f32[144,128]{1,0:T(8,128)} %get-tuple-element.58) | copy-start | bytes 221188
  216.1 5.7 %copy-start.2 = (f32[576,128]{1,0:T(8,128)S(1)}, f32[576,128]{1,0:T(8,128)}, u32[]{:S(2)}) copy-start(f32[576,128]{1,0:T(8,128)} %get-tuple-element.60) | copy-start | bytes 884740
  216.1 6.4 %copy-start.3 = (f32[144,128]{1,0:T(8,128)S(1)}, f32[144,128]{1,0:T(8,128)}, u32[]{:S(2)}) copy-start(f32[144,128]{1,0:T(8,128)} %get-tuple-element.61) | copy-start | bytes 221188
